TPU v7x, 32 devices: a whole 2x2x4 slice. The times are simulated.
32 devices in a mesh: px: 4 (over z), py: 8 (over y, x, core).
Axes of the slice: x: 2, y: 2, z: 4, core: 2. Of those that a mesh axis runs over, the one named last changes fastest.
Arguments:
- background_field: float32 [32, 256, 1024], P('px', 'py'), may hold values from -6 to 6
- perturbation: float32 [32, 256, 1024], P('px', 'py'), may hold values from -6 to 6
- permittivity: float32 [32, 256, 1024], P('px', 'py'), may hold values from 0.5 to 2
- probe_nodes: int32 [4, 32768], P(None, ('px', 'py')), may hold values from 0 to 262143
- probe_weights: float32 [4, 32768], P(None, ('px', 'py')), may hold values from 0.1 to 1
- probe_owner: int32 [32768, 1], P(('px', 'py')), may hold values from 0 to 31; in each aligned block of 1024 rows (0 to 1023, 1024 to 2047, ...) at most 64 rows name the same one
- probe_sensor: int32 [32768], P(('px', 'py')), may hold values from 0 to 7
- sensor_weight: float32 [256], P(('px', 'py')), may hold values from 0.2 to 5
Outputs:
- hess_vec: float32 [32, 256, 1024], P('px', 'py')
Inputs may be any that keep to these rules, and one draw needn't show every extreme that they name: `probe_nodes`: each probe's nodes lie in the block of the device that holds the probe. `probe_owner`: of the probes of one device at most 64 name the same owner, and in every draw some owner is named by exactly 64 of them.
All inputs are finite; a program needn't handle non-finite values.
Results may differ from a plain program's by a relative error of at most 0.00025.
Values sent between devices are 32-bit elements; how exact they have to be, the bound alone decides.
A program may use at most 64 MiB of HBM per device.

v0:
```python
import jax
import jax.numpy as jnp
from jax import lax
from jax.sharding import PartitionSpec as P

SWEEPS = 4


mass_term = 1.0
bound_low = 1.0
bound_high = 25.0


def padded_2(block, sides, width):
    for axis, dim in sides:
        count = lax.axis_size(axis)
        forward = [(i, i + 1) for i in range(count - 1)]
        backward = [(target, source) for source, target in forward]
        low = lax.ppermute(
            lax.slice_in_dim(block, block.shape[dim] - width, None, axis=dim), axis, forward
        )
        high = lax.ppermute(lax.slice_in_dim(block, 0, width, axis=dim), axis, backward)
        block = jnp.concatenate([low, block, high], axis=dim)
    return block


def crop_rim(array, depth):
    return array[depth : array.shape[0] - depth, depth : array.shape[1] - depth]


def inside_line(count, index, total, depth):
    positions = index * count - depth + jnp.arange(count + 2 * depth, dtype=jnp.int32)
    return ((positions >= 0) & (positions < total)).astype(jnp.float32)


def face_masks(row_inside, col_inside):
    row_faces = (row_inside[1:] * row_inside[:-1])[:, None] * col_inside[None, :]
    col_faces = row_inside[:, None] * (col_inside[1:] * col_inside[:-1])[None, :]
    return (row_faces, col_faces)


def face_coefs(padded, row_inside, col_inside):
    row_faces, col_faces = face_masks(row_inside, col_inside)
    cell_inside = row_inside[:, None] * col_inside[None, :]
    along_rows = 0.5 * (padded[1:] + padded[:-1]) * row_faces[:, :, None]
    along_cols = 0.5 * (padded[:, 1:] + padded[:, :-1]) * col_faces[:, :, None]
    along_depth = 0.5 * (padded[:, :, 1:] + padded[:, :, :-1]) * cell_inside[:, :, None]
    return (along_rows, along_cols, along_depth)


def apply_local(field, coefs, mass_value, depth):
    along_rows = crop_rim(coefs[0], depth)
    along_cols = crop_rim(coefs[1], depth)
    along_depth = crop_rim(coefs[2], depth + 1)
    inner = field[1:-1, 1:-1]
    row_flux = along_rows[:, 1:-1] * (field[1:, 1:-1] - field[:-1, 1:-1])
    col_flux = along_cols[1:-1] * (field[1:-1, 1:] - field[1:-1, :-1])
    depth_flux = along_depth * (inner[:, :, 1:] - inner[:, :, :-1])
    zero_plane = jnp.zeros_like(depth_flux[:, :, :1])
    result = mass_value * inner - row_flux[1:] + row_flux[:-1] - col_flux[:, 1:] + col_flux[:, :-1]
    return (
        result
        - jnp.concatenate([depth_flux, zero_plane], 2)
        + jnp.concatenate([zero_plane, depth_flux], 2)
    )


def cheb_constants():
    centre = 0.5 * (bound_high + bound_low)
    half_width = 0.5 * (bound_high - bound_low)
    return (centre, half_width, centre / half_width)


def solve_faces(source, coefs):
    centre, half_width, spread = cheb_constants()
    iterate = jnp.zeros_like(source)
    remain = source
    search = source / centre
    ratio_now = 1.0 / spread
    for sweep in range(SWEEPS):
        iterate = iterate + search
        if sweep < SWEEPS - 1:
            search_pad = padded_2(search, (("px", 0), ("py", 1)), 1)
            remain = remain - apply_local(search_pad, coefs, mass_term, 0)
            ratio_next = 1.0 / (2.0 * spread - ratio_now)
            search = ratio_next * ratio_now * search + 2.0 * ratio_next / half_width * remain
            ratio_now = ratio_next
    return iterate


def sensitivity(back_pad, adj_pad, row_inside, col_inside):
    row_faces, col_faces = face_masks(row_inside, col_inside)
    row_term = (
        row_faces[:, 1:-1, None]
        * (back_pad[1:, 1:-1] - back_pad[:-1, 1:-1])
        * (adj_pad[1:, 1:-1] - adj_pad[:-1, 1:-1])
    )
    col_term = (
        col_faces[1:-1, :, None]
        * (back_pad[1:-1, 1:] - back_pad[1:-1, :-1])
        * (adj_pad[1:-1, 1:] - adj_pad[1:-1, :-1])
    )
    inner_back = back_pad[1:-1, 1:-1]
    inner_adj = adj_pad[1:-1, 1:-1]
    depth_term = (inner_back[:, :, 1:] - inner_back[:, :, :-1]) * (
        inner_adj[:, :, 1:] - inner_adj[:, :, :-1]
    )
    zero_plane = jnp.zeros_like(depth_term[:, :, :1])
    total = row_term[1:] + row_term[:-1] + col_term[:, 1:] + col_term[:, :-1]
    total = (
        total
        + jnp.concatenate([depth_term, zero_plane], 2)
        + jnp.concatenate([zero_plane, depth_term], 2)
    )
    return -0.5 * total


def body(
    background_field,
    perturbation,
    permittivity,
    probe_nodes,
    probe_weights,
    probe_owner,
    probe_sensor,
    sensor_weight,
):
    rows_dev, cols_dev, depth_dev = background_field.shape
    size_px = lax.axis_size("px")
    size_py = lax.axis_size("py")
    index_px = lax.axis_index("px")
    index_py = lax.axis_index("py")
    rows_one = inside_line(rows_dev, index_px, rows_dev * size_px, 1)
    cols_one = inside_line(cols_dev, index_py, cols_dev * size_py, 1)
    back_pad, perturb_pad, permit_pad = (
        padded_2(background_field, (("px", 0), ("py", 1)), 1),
        padded_2(perturbation, (("px", 0), ("py", 1)), 1),
        padded_2(permittivity, (("px", 0), ("py", 1)), 1),
    )
    permit_coefs = face_coefs(permit_pad, rows_one, cols_one)

    def solve_field(source):
        return solve_faces(source, permit_coefs)

    perturb_coefs = face_coefs(perturb_pad, rows_one, cols_one)
    tangent = solve_field(-apply_local(back_pad, perturb_coefs, 0.0, 0))
    flat = tangent.reshape(-1)
    values = jnp.sum(probe_weights * flat[probe_nodes], axis=0)
    owner_ids = probe_owner[:, 0]
    sensors_dev = sensor_weight.shape[0]
    device_count = size_px * size_py
    probes = probe_sensor.shape[0]
    capacity = max(2, 2 * probes // device_count)
    owner_hot = (owner_ids[:, None] == jnp.arange(device_count, dtype=jnp.int32)[None, :]).astype(
        jnp.int32
    )
    before_count = jnp.sum((jnp.cumsum(owner_hot, axis=0) - owner_hot) * owner_hot, axis=1)
    slot_index = owner_ids * capacity + before_count
    send_values = (
        jnp.zeros((device_count * capacity,), jnp.float32)
        .at[slot_index]
        .set(values)
        .reshape(device_count, capacity)
    )
    send_sensor = (
        jnp.zeros((device_count * capacity,), jnp.int32)
        .at[slot_index]
        .set(probe_sensor)
        .reshape(device_count, capacity)
    )
    got_values, got_sensor = (
        lax.all_to_all(send_values, ("px", "py"), split_axis=0, concat_axis=0, tiled=True),
        lax.all_to_all(send_sensor, ("px", "py"), split_axis=0, concat_axis=0, tiled=True),
    )
    sensor_hot = (
        got_sensor[:, :, None] == jnp.arange(sensors_dev, dtype=jnp.int32)[None, None, :]
    ).astype(jnp.float32)
    readings = jnp.einsum("dcs,dc->s", sensor_hot, got_values, precision=lax.Precision.HIGHEST)
    weighted = readings * sensor_weight
    reply = jnp.einsum("dcs,s->dc", sensor_hot, weighted, precision=lax.Precision.HIGHEST)
    back_values = lax.all_to_all(reply, ("px", "py"), split_axis=0, concat_axis=0, tiled=True)
    returned = back_values.reshape(-1)[slot_index]
    source = (
        jnp.zeros(flat.shape, jnp.float32)
        .at[probe_nodes.reshape(-1)]
        .add((probe_weights * returned[None, :]).reshape(-1))
    )
    adjoint = solve_field(source.reshape(tangent.shape))
    adj_pad = padded_2(adjoint, (("px", 0), ("py", 1)), 1)
    return sensitivity(back_pad, adj_pad, rows_one, cols_one)


def solution(mesh):
    placed = (
        P("px", "py", None),
        P("px", "py", None),
        P("px", "py", None),
        P(None, ("px", "py")),
        P(None, ("px", "py")),
        P(("px", "py"), None),
        P(("px", "py")),
        P(("px", "py")),
    )
    return jax.shard_map(
        body, mesh=mesh, in_specs=placed, out_specs=P("px", "py", None), check_vma=False
    )
```

profile of v0, /device:TPU:27, one launch (start us, length us, event | category | flops | bytes accessed | tf_op | source)
XLA Modules:
  0.0 312.0 jit_solution(13885707921617575100)
XLA Ops:
  0.9 9.0 %reduce-window.6 = s32[32,8,128]{2,1,0:T(8,128)S(1)} reduce-window(s32[32,8,128]{2,1,0:T(8,128)S(1)} %fusion.79, s32[]{:T(128)} %constant.23.clone.1), window={size=1x1x128 pad=0_0x0_0x127_0}, to_apply=%region_0.0 | reduce-window | flops 4161536 | bytes 262148 | tf_op jit(solution)/shard_map/reduce-window
  11.9 4.5 %scatter_custom_fusion = s32[2048]{0:T(1024)S(1)} fusion(s32[1024]{0:T(1024)S(1)} %bitcast.67, s32[1024]{0:T(1024)} %param.14, s32[]{:T(128)} %constant.23.clone.1), kind=kCustom, calls=%fused_computation.244 | custom fusion | bytes 8704 | tf_op jit(solution)/shard_map/scatter | solution.py:168
  17.0 6.2 %all-to-all-start = ((s32[32,1,64]{2,1,0:T(1,128)}), s32[32,1,64]{2,1,0:T(1,128)}, u32[]{:S(2)}, u32[]{:S(2)}) async-start(s32[32,1,64]{2,1,0:T(1,128)} %all_to_all.20), calls=%async_computation | async-start | bytes 32768 | tf_op jit(solution)/shard_map/all_to_all | solution.py:173
  26.2 4.6 %collective-permute-start.3 = (f32[1,32,1024]{2,1,0:T(8,128)}, f32[1,32,1024]{2,1,0:T(8,128)}, u32[]{:S(2)}, u32[]{:S(2)}) collective-permute-start(f32[1,32,1024]{2,1,0:T(8,128)} %get-tuple-element.65), channel_id=1, source_target_pairs={{8,0},{16,8},{24,16},{9,1},{17,9},{25,17},{10,2},{18,10},{26,18},{... | collective-permute-start | bytes 393224 | tf_op jit(solution)/shard_map/ppermute | solution.py:22
  32.9 4.0 %collective-permute-start = (f32[1,32,1024]{2,1,0:T(8,128)}, f32[1,32,1024]{2,1,0:T(8,128)S(1)}, u32[]{:S(2)}, u32[]{:S(2)}) collective-permute-start(f32[1,32,1024]{2,1,0:T(8,128)} %get-tuple-element.63), channel_id=1, source_target_pairs={{8,0},{16,8},{24,16},{9,1},{17,9},{25,17},{10,2},{18,10},{26,18},{... | collective-permute-start | bytes 393224 | tf_op jit(solution)/shard_map/ppermute | solution.py:22
  41.9 4.0 %collective-permute-start.9 = (f32[1,32,1024]{2,1,0:T(8,128)}, f32[1,32,1024]{2,1,0:T(8,128)S(1)}, u32[]{:S(2)}, u32[]{:S(2)}) collective-permute-start(f32[1,32,1024]{2,1,0:T(8,128)} %get-tuple-element.61), channel_id=1, source_target_pairs={{8,0},{16,8},{24,16},{9,1},{17,9},{25,17},{10,2},{18,10},{26,18},{... | collective-permute-start | bytes 393224 | tf_op jit(solution)/shard_map/ppermute | solution.py:22
  47.9 3.9 %collective-permute-start.5 = (f32[10,1,1024]{2,1,0:T(1,128)S(1)}, f32[10,1,1024]{2,1,0:T(1,128)S(1)}, u32[]{:S(2)}, u32[]{:S(2)}) collective-permute-start(f32[10,1,1024]{2,1,0:T(1,128)S(1)} %get-tuple-element.46), channel_id=1, source_target_pairs={{1,0},{2,1},{3,2},{4,3},{5,4},{6,5},{7,6},{9,8},{10,9},{11,10},{12... | collective-permute-start | bytes 122888 | tf_op jit(solution)/shard_map/ppermute | solution.py:22
  51.9 3.0 collective-permute-start.4
  55.1 2.4 collective-permute-start.7
  60.6 2.6 collective-permute-start.11
  63.2 3.9 %collective-permute-start.10 = (f32[10,1,1024]{2,1,0:T(1,128)S(1)}, f32[10,1,1024]{2,1,0:T(1,128)S(1)}, u32[]{:S(2)}, u32[]{:S(2)}) collective-permute-start(f32[10,1,1024]{2,1,0:T(1,128)S(1)} %get-tuple-element.41), channel_id=1, source_target_pairs={{0,1},{1,2},{2,3},{3,4},{4,5},{5,6},{6,7},{8,9},{9,10},{10,11},{11... | collective-permute-start | bytes 122888 | tf_op jit(solution)/shard_map/ppermute | solution.py:19
  76.5 3.8 %collective-permute-done.13 = f32[1,32,1024]{2,1,0:T(8,128)S(1)} collective-permute-done((f32[1,32,1024]{2,1,0:T(8,128)S(1)}, f32[1,32,1024]{2,1,0:T(8,128)S(1)}, u32[]{:S(2)}, u32[]{:S(2)}) %collective-permute-start.13) | collective-permute-done | bytes 131104 | tf_op jit(solution)/shard_map/ppermute | solution.py:19
  80.4 5.3 %collective-permute-start.15 = (f32[10,1,1024]{2,1,0:T(1,128)S(1)}, f32[10,1,1024]{2,1,0:T(1,128)S(1)}, u32[]{:S(2)}, u32[]{:S(2)}) collective-permute-start(f32[10,1,1024]{2,1,0:T(1,128)S(1)} %get-tuple-element.40), channel_id=1, source_target_pairs={{0,1},{1,2},{2,3},{3,4},{4,5},{5,6},{6,7},{8,9},{9,10},{10,11},{11... | collective-permute-start | bytes 122888 | tf_op jit(solution)/shard_map/ppermute | solution.py:19
  85.7 1.9 collective-permute-start.14
  88.1 3.8 %collective-permute-done.14 = f32[10,1,1024]{2,1,0:T(1,128)S(1)} collective-permute-done((f32[10,1,1024]{2,1,0:T(1,128)S(1)}, f32[10,1,1024]{2,1,0:T(1,128)S(1)}, u32[]{:S(2)}, u32[]{:S(2)}) %collective-permute-start.14) | collective-permute-done | bytes 40992 | tf_op jit(solution)/shard_map/ppermute | solution.py:22
  93.3 3.3 %collective-permute-start.16 = (f32[1,32,1024]{2,1,0:T(8,128)S(1)}, f32[1,32,1024]{2,1,0:T(8,128)S(1)}, u32[]{:S(2)}, u32[]{:S(2)}) collective-permute-start(f32[1,32,1024]{2,1,0:T(8,128)S(1)} %get-tuple-element.58), channel_id=1, source_target_pairs={{8,0},{16,8},{24,16},{9,1},{17,9},{25,17},{10,2},{18,10},{26,18},{... | collective-permute-start | bytes 393224 | tf_op jit(solution)/shard_map/ppermute | solution.py:22
  98.5 3.8 %collective-permute-done.17 = f32[1,32,1024]{2,1,0:T(8,128)S(1)} collective-permute-done((f32[1,32,1024]{2,1,0:T(8,128)S(1)}, f32[1,32,1024]{2,1,0:T(8,128)S(1)}, u32[]{:S(2)}, u32[]{:S(2)}) %collective-permute-start.17) | collective-permute-done | bytes 131104 | tf_op jit(solution)/shard_map/ppermute | solution.py:19
  102.3 3.3 %collective-permute-start.19 = (f32[10,1,1024]{2,1,0:T(1,128)S(1)}, f32[10,1,1024]{2,1,0:T(1,128)S(1)}, u32[]{:S(2)}, u32[]{:S(2)}) collective-permute-start(f32[10,1,1024]{2,1,0:T(1,128)S(1)} %get-tuple-element.38), channel_id=1, source_target_pairs={{0,1},{1,2},{2,3},{3,4},{4,5},{5,6},{6,7},{8,9},{9,10},{10,11},{11... | collective-permute-start | bytes 122888 | tf_op jit(solution)/shard_map/ppermute | solution.py:19
  105.7 2.1 collective-permute-start.18
  108.1 3.8 %collective-permute-done.18 = f32[10,1,1024]{2,1,0:T(1,128)S(1)} collective-permute-done((f32[10,1,1024]{2,1,0:T(1,128)S(1)}, f32[10,1,1024]{2,1,0:T(1,128)S(1)}, u32[]{:S(2)}, u32[]{:S(2)}) %collective-permute-start.18) | collective-permute-done | bytes 40992 | tf_op jit(solution)/shard_map/ppermute | solution.py:22
  116.9 3.8 %collective-permute-done.21 = f32[1,32,1024]{2,1,0:T(8,128)S(1)} collective-permute-done((f32[1,32,1024]{2,1,0:T(8,128)S(1)}, f32[1,32,1024]{2,1,0:T(8,128)S(1)}, u32[]{:S(2)}, u32[]{:S(2)}) %collective-permute-start.21) | collective-permute-done | bytes 131104 | tf_op jit(solution)/shard_map/ppermute | solution.py:19
  120.7 3.3 %collective-permute-start.23 = (f32[10,1,1024]{2,1,0:T(1,128)S(1)}, f32[10,1,1024]{2,1,0:T(1,128)S(1)}, u32[]{:S(2)}, u32[]{:S(2)}) collective-permute-start(f32[10,1,1024]{2,1,0:T(1,128)S(1)} %get-tuple-element.36), channel_id=1, source_target_pairs={{0,1},{1,2},{2,3},{3,4},{4,5},{5,6},{6,7},{8,9},{9,10},{10,11},{11... | collective-permute-start | bytes 122888 | tf_op jit(solution)/shard_map/ppermute | solution.py:19
  126.3 4.0 %collective-permute-done.22 = f32[10,1,1024]{2,1,0:T(1,128)S(1)} collective-permute-done((f32[10,1,1024]{2,1,0:T(1,128)S(1)}, f32[10,1,1024]{2,1,0:T(1,128)S(1)}, u32[]{:S(2)}, u32[]{:S(2)}) %collective-permute-start.22) | collective-permute-done | bytes 40992 | tf_op jit(solution)/shard_map/ppermute | solution.py:22
  132.0 40.7 %gather_fusion = f32[4096]{0:T(1024)} fusion(f32[262144]{0:T(1024)S(1)} %bitcast.58, s32[4096]{0:T(1024)} %bitcast_clamp_fusion), kind=kCustom, calls=%fused_computation | custom fusion | bytes 49152 | tf_op jit(solution)/shard_map/gather | solution.py:148
  173.4 4.3 %scatter_custom_fusion.1 = f32[2048]{0:T(1024)S(1)} fusion(s32[1024]{0:T(1024)S(1)} %bitcast.68, f32[1024]{0:T(1024)S(1)} %multiply_reduce_fusion, f32[]{:T(128)} %constant.27.clone.1), kind=kCustom, calls=%fused_computation.242 | custom fusion | bytes 8196 | tf_op jit(solution)/shard_map/scatter | solution.py:162
  178.4 4.7 %all-to-all-start.1 = ((f32[32,1,64]{2,1,0:T(1,128)}), f32[32,1,64]{2,1,0:T(1,128)S(1)}, u32[]{:S(2)}, u32[]{:S(2)}) async-start(f32[32,1,64]{2,1,0:T(1,128)} %all_to_all.22), calls=%async_computation.1 | async-start | bytes 32768 | tf_op jit(solution)/shard_map/all_to_all | solution.py:172
  183.8 2.0 all-to-all-done.1
  187.1 2.7 convolution_bitcast_fusion
  189.9 6.9 %all-to-all-start.2 = ((f32[32,1,64]{2,1,0:T(1,128)}), f32[32,1,64]{2,1,0:T(1,128)S(1)}, u32[]{:S(2)}, u32[]{:S(2)}) async-start(f32[32,1,64]{2,1,0:T(1,128)} %convolution_bitcast_fusion), calls=%async_computation.2 | async-start | bytes 32768 | tf_op jit(solution)/shard_map/all_to_all | solution.py:181
  200.8 6.1 %gather_fusion.1 = f32[1024]{0:T(1024)S(1)} fusion(f32[2048]{0:T(1024)S(1)} %reshape.175, s32[1024]{0:T(1024)S(1)} %broadcast_clamp_fusion), kind=kCustom, calls=%fused_computation.1 | custom fusion | bytes 12288 | tf_op jit(solution)/shard_map/gather | solution.py:182
  207.0 22.9 %scatter_custom_fusion.2 = f32[262144]{0:T(1024)} fusion(s32[4096]{0:T(1024)S(1)} %bitcast.70, f32[4096]{0:T(1024)S(1)} %bitcast.71, f32[]{:T(128)} %constant.27.clone.1), kind=kCustom, calls=%fused_computation.189 | custom fusion | flops 4096 | bytes 1048580 | tf_op jit(solution)/shard_map/scatter-add | solution.py:186
  231.4 3.3 %collective-permute-start.24 = (f32[1,32,1024]{2,1,0:T(8,128)S(1)}, f32[1,32,1024]{2,1,0:T(8,128)S(1)}, u32[]{:S(2)}, u32[]{:S(2)}) collective-permute-start(f32[1,32,1024]{2,1,0:T(8,128)S(1)} %get-tuple-element.54), channel_id=1, source_target_pairs={{8,0},{16,8},{24,16},{9,1},{17,9},{25,17},{10,2},{18,10},{26,18},{... | collective-permute-start | bytes 393224 | tf_op jit(solution)/shard_map/ppermute | solution.py:22
  236.9 3.5 %collective-permute-done.25 = f32[1,32,1024]{2,1,0:T(8,128)S(1)} collective-permute-done((f32[1,32,1024]{2,1,0:T(8,128)S(1)}, f32[1,32,1024]{2,1,0:T(8,128)S(1)}, u32[]{:S(2)}, u32[]{:S(2)}) %collective-permute-start.25) | collective-permute-done | bytes 131104 | tf_op jit(solution)/shard_map/ppermute | solution.py:19
  240.5 5.1 %collective-permute-start.27 = (f32[10,1,1024]{2,1,0:T(1,128)S(1)}, f32[10,1,1024]{2,1,0:T(1,128)S(1)}, u32[]{:S(2)}, u32[]{:S(2)}) collective-permute-start(f32[10,1,1024]{2,1,0:T(1,128)S(1)} %get-tuple-element.34), channel_id=1, source_target_pairs={{0,1},{1,2},{2,3},{3,4},{4,5},{5,6},{6,7},{8,9},{9,10},{10,11},{11... | collective-permute-start | bytes 122888 | tf_op jit(solution)/shard_map/ppermute | solution.py:19
  247.7 4.0 %collective-permute-done.26 = f32[10,1,1024]{2,1,0:T(1,128)S(1)} collective-permute-done((f32[10,1,1024]{2,1,0:T(1,128)S(1)}, f32[10,1,1024]{2,1,0:T(1,128)S(1)}, u32[]{:S(2)}, u32[]{:S(2)}) %collective-permute-start.26) | collective-permute-done | bytes 40992 | tf_op jit(solution)/shard_map/ppermute | solution.py:22
  253.0 3.1 collective-permute-start.28
  258.0 4.0 %collective-permute-done.29 = f32[1,32,1024]{2,1,0:T(8,128)S(1)} collective-permute-done((f32[1,32,1024]{2,1,0:T(8,128)S(1)}, f32[1,32,1024]{2,1,0:T(8,128)S(1)}, u32[]{:S(2)}, u32[]{:S(2)}) %collective-permute-start.29) | collective-permute-done | bytes 131104 | tf_op jit(solution)/shard_map/ppermute | solution.py:19
  262.0 3.1 %collective-permute-start.31 = (f32[10,1,1024]{2,1,0:T(1,128)S(1)}, f32[10,1,1024]{2,1,0:T(1,128)S(1)}, u32[]{:S(2)}, u32[]{:S(2)}) collective-permute-start(f32[10,1,1024]{2,1,0:T(1,128)S(1)} %get-tuple-element.32), channel_id=1, source_target_pairs={{0,1},{1,2},{2,3},{3,4},{4,5},{5,6},{6,7},{8,9},{9,10},{10,11},{11... | collective-permute-start | bytes 122888 | tf_op jit(solution)/shard_map/ppermute | solution.py:19
  265.2 2.1 collective-permute-start.30
  267.6 3.8 %collective-permute-done.30 = f32[10,1,1024]{2,1,0:T(1,128)S(1)} collective-permute-done((f32[10,1,1024]{2,1,0:T(1,128)S(1)}, f32[10,1,1024]{2,1,0:T(1,128)S(1)}, u32[]{:S(2)}, u32[]{:S(2)}) %collective-permute-start.30) | collective-permute-done | bytes 40992 | tf_op jit(solution)/shard_map/ppermute | solution.py:22
  272.8 3.1 collective-permute-start.32
  277.8 3.8 %collective-permute-done.33 = f32[1,32,1024]{2,1,0:T(8,128)S(1)} collective-permute-done((f32[1,32,1024]{2,1,0:T(8,128)S(1)}, f32[1,32,1024]{2,1,0:T(8,128)S(1)}, u32[]{:S(2)}, u32[]{:S(2)}) %collective-permute-start.33) | collective-permute-done | bytes 131104 | tf_op jit(solution)/shard_map/ppermute | solution.py:19
  281.7 3.3 %collective-permute-start.35 = (f32[10,1,1024]{2,1,0:T(1,128)S(1)}, f32[10,1,1024]{2,1,0:T(1,128)S(1)}, u32[]{:S(2)}, u32[]{:S(2)}) collective-permute-start(f32[10,1,1024]{2,1,0:T(1,128)S(1)} %get-tuple-element.30), channel_id=1, source_target_pairs={{0,1},{1,2},{2,3},{3,4},{4,5},{5,6},{6,7},{8,9},{9,10},{10,11},{11... | collective-permute-start | bytes 122888 | tf_op jit(solution)/shard_map/ppermute | solution.py:19
  287.3 4.0 %collective-permute-done.34 = f32[10,1,1024]{2,1,0:T(1,128)S(1)} collective-permute-done((f32[10,1,1024]{2,1,0:T(1,128)S(1)}, f32[10,1,1024]{2,1,0:T(1,128)S(1)}, u32[]{:S(2)}, u32[]{:S(2)}) %collective-permute-start.34) | collective-permute-done | bytes 40992 | tf_op jit(solution)/shard_map/ppermute | solution.py:22
  296.5 3.8 %collective-permute-done.37 = f32[1,32,1024]{2,1,0:T(8,128)S(1)} collective-permute-done((f32[1,32,1024]{2,1,0:T(8,128)S(1)}, f32[1,32,1024]{2,1,0:T(8,128)S(1)}, u32[]{:S(2)}, u32[]{:S(2)}) %collective-permute-start.37) | collective-permute-done | bytes 131104 | tf_op jit(solution)/shard_map/ppermute | solution.py:19
  300.4 3.3 %collective-permute-start.39 = (f32[10,1,1024]{2,1,0:T(1,128)S(1)}, f32[10,1,1024]{2,1,0:T(1,128)S(1)}, u32[]{:S(2)}, u32[]{:S(2)}) collective-permute-start(f32[10,1,1024]{2,1,0:T(1,128)S(1)} %get-tuple-element.28), channel_id=1, source_target_pairs={{0,1},{1,2},{2,3},{3,4},{4,5},{5,6},{6,7},{8,9},{9,10},{10,11},{11... | collective-permute-start | bytes 122888 | tf_op jit(solution)/shard_map/ppermute | solution.py:19
  303.7 2.1 collective-permute-start.38
  306.1 4.0 %collective-permute-done.38 = f32[10,1,1024]{2,1,0:T(1,128)S(1)} collective-permute-done((f32[10,1,1024]{2,1,0:T(1,128)S(1)}, f32[10,1,1024]{2,1,0:T(1,128)S(1)}, u32[]{:S(2)}, u32[]{:S(2)}) %collective-permute-start.38) | collective-permute-done | bytes 40992 | tf_op jit(solution)/shard_map/ppermute | solution.py:22
  (189 shorter events, 70.7 us)
Async XLA Ops:
  0.0 36.9 %copy-start.8 = (f32[8,32,1024]{2,1,0:T(8,128)S(1)}, f32[8,32,1024]{2,1,0:T(8,128)}, u32[]{:S(2)}) copy-start(f32[8,32,1024]{2,1,0:T(8,128)} %param.10) | copy-start | bytes 3145732
  10.1 36.7 %copy-start.7 = (f32[8,32,1024]{2,1,0:T(8,128)S(1)}, f32[8,32,1024]{2,1,0:T(8,128)}, u32[]{:S(2)}) copy-start(f32[8,32,1024]{2,1,0:T(8,128)} %param.9) | copy-start | bytes 3145732
  17.0 161.4 %all-to-all-start = ((s32[32,1,64]{2,1,0:T(1,128)}), s32[32,1,64]{2,1,0:T(1,128)}, u32[]{:S(2)}, u32[]{:S(2)}) async-start(s32[32,1,64]{2,1,0:T(1,128)} %all_to_all.20), calls=%async_computation | async-start | bytes 32768 | tf_op jit(solution)/shard_map/all_to_all | solution.py:173
  24.9 17.0 %collective-permute-start.2 = (f32[1,32,1024]{2,1,0:T(8,128)}, f32[1,32,1024]{2,1,0:T(8,128)}, u32[]{:S(2)}, u32[]{:S(2)}) collective-permute-start(f32[1,32,1024]{2,1,0:T(8,128)} %get-tuple-element.66), channel_id=1, source_target_pairs={{0,8},{8,16},{16,24},{1,9},{9,17},{17,25},{2,10},{10,18},{18,26},{... | collective-permute-start | bytes 393224 | tf_op jit(solution)/shard_map/ppermute | solution.py:19
  26.2 20.7 %collective-permute-start.3 = (f32[1,32,1024]{2,1,0:T(8,128)}, f32[1,32,1024]{2,1,0:T(8,128)}, u32[]{:S(2)}, u32[]{:S(2)}) collective-permute-start(f32[1,32,1024]{2,1,0:T(8,128)} %get-tuple-element.65), channel_id=1, source_target_pairs={{8,0},{16,8},{24,16},{9,1},{17,9},{25,17},{10,2},{18,10},{26,18},{... | collective-permute-start | bytes 393224 | tf_op jit(solution)/shard_map/ppermute | solution.py:22
  31.6 20.2 %collective-permute-start.1 = (f32[1,32,1024]{2,1,0:T(8,128)}, f32[1,32,1024]{2,1,0:T(8,128)S(1)}, u32[]{:S(2)}, u32[]{:S(2)}) collective-permute-start(f32[1,32,1024]{2,1,0:T(8,128)} %get-tuple-element.64), channel_id=1, source_target_pairs={{0,8},{8,16},{16,24},{1,9},{9,17},{17,25},{2,10},{10,18},{18,26},{... | collective-permute-start | bytes 393224 | tf_op jit(solution)/shard_map/ppermute | solution.py:19
  32.9 22.1 %collective-permute-start = (f32[1,32,1024]{2,1,0:T(8,128)}, f32[1,32,1024]{2,1,0:T(8,128)S(1)}, u32[]{:S(2)}, u32[]{:S(2)}) collective-permute-start(f32[1,32,1024]{2,1,0:T(8,128)} %get-tuple-element.63), channel_id=1, source_target_pairs={{8,0},{16,8},{24,16},{9,1},{17,9},{25,17},{10,2},{18,10},{26,18},{... | collective-permute-start | bytes 393224 | tf_op jit(solution)/shard_map/ppermute | solution.py:22
  37.6 19.9 %collective-permute-start.8 = (f32[1,32,1024]{2,1,0:T(8,128)}, f32[1,32,1024]{2,1,0:T(8,128)}, u32[]{:S(2)}, u32[]{:S(2)}) collective-permute-start(f32[1,32,1024]{2,1,0:T(8,128)} %get-tuple-element.62), channel_id=1, source_target_pairs={{0,8},{8,16},{16,24},{1,9},{9,17},{17,25},{2,10},{10,18},{18,26},{... | collective-permute-start | bytes 393224 | tf_op jit(solution)/shard_map/ppermute | solution.py:19
  41.9 18.6 %collective-permute-start.9 = (f32[1,32,1024]{2,1,0:T(8,128)}, f32[1,32,1024]{2,1,0:T(8,128)S(1)}, u32[]{:S(2)}, u32[]{:S(2)}) collective-permute-start(f32[1,32,1024]{2,1,0:T(8,128)} %get-tuple-element.61), channel_id=1, source_target_pairs={{8,0},{16,8},{24,16},{9,1},{17,9},{25,17},{10,2},{18,10},{26,18},{... | collective-permute-start | bytes 393224 | tf_op jit(solution)/shard_map/ppermute | solution.py:22
  47.9 15.3 %collective-permute-start.5 = (f32[10,1,1024]{2,1,0:T(1,128)S(1)}, f32[10,1,1024]{2,1,0:T(1,128)S(1)}, u32[]{:S(2)}, u32[]{:S(2)}) collective-permute-start(f32[10,1,1024]{2,1,0:T(1,128)S(1)} %get-tuple-element.46), channel_id=1, source_target_pairs={{1,0},{2,1},{3,2},{4,3},{5,4},{6,5},{7,6},{9,8},{10,9},{11,10},{12... | collective-permute-start | bytes 122888 | tf_op jit(solution)/shard_map/ppermute | solution.py:22
  51.9 15.3 %collective-permute-start.4 = (f32[10,1,1024]{2,1,0:T(1,128)S(1)}, f32[10,1,1024]{2,1,0:T(1,128)S(1)}, u32[]{:S(2)}, u32[]{:S(2)}) collective-permute-start(f32[10,1,1024]{2,1,0:T(1,128)S(1)} %get-tuple-element.45), channel_id=1, source_target_pairs={{0,1},{1,2},{2,3},{3,4},{4,5},{5,6},{6,7},{8,9},{9,10},{10,11},{11... | collective-permute-start | bytes 122888 | tf_op jit(solution)/shard_map/ppermute | solution.py:19
  55.1 14.8 %collective-permute-start.7 = (f32[10,1,1024]{2,1,0:T(1,128)S(1)}, f32[10,1,1024]{2,1,0:T(1,128)S(1)}, u32[]{:S(2)}, u32[]{:S(2)}) collective-permute-start(f32[10,1,1024]{2,1,0:T(1,128)S(1)} %get-tuple-element.44), channel_id=1, source_target_pairs={{0,1},{1,2},{2,3},{3,4},{4,5},{5,6},{6,7},{8,9},{9,10},{10,11},{11... | collective-permute-start | bytes 122888 | tf_op jit(solution)/shard_map/ppermute | solution.py:19
  57.6 12.4 %collective-permute-start.6 = (f32[10,1,1024]{2,1,0:T(1,128)S(1)}, f32[10,1,1024]{2,1,0:T(1,128)S(1)}, u32[]{:S(2)}, u32[]{:S(2)}) collective-permute-start(f32[10,1,1024]{2,1,0:T(1,128)S(1)} %get-tuple-element.43), channel_id=1, source_target_pairs={{1,0},{2,1},{3,2},{4,3},{5,4},{6,5},{7,6},{9,8},{10,9},{11,10},{12... | collective-permute-start | bytes 122888 | tf_op jit(solution)/shard_map/ppermute | solution.py:22
  60.6 7.8 %collective-permute-start.11 = (f32[10,1,1024]{2,1,0:T(1,128)S(1)}, f32[10,1,1024]{2,1,0:T(1,128)S(1)}, u32[]{:S(2)}, u32[]{:S(2)}) collective-permute-start(f32[10,1,1024]{2,1,0:T(1,128)S(1)} %get-tuple-element.42), channel_id=1, source_target_pairs={{1,0},{2,1},{3,2},{4,3},{5,4},{6,5},{7,6},{9,8},{10,9},{11,10},{12... | collective-permute-start | bytes 122888 | tf_op jit(solution)/shard_map/ppermute | solution.py:22
  63.2 5.3 %collective-permute-start.10 = (f32[10,1,1024]{2,1,0:T(1,128)S(1)}, f32[10,1,1024]{2,1,0:T(1,128)S(1)}, u32[]{:S(2)}, u32[]{:S(2)}) collective-permute-start(f32[10,1,1024]{2,1,0:T(1,128)S(1)} %get-tuple-element.41), channel_id=1, source_target_pairs={{0,1},{1,2},{2,3},{3,4},{4,5},{5,6},{6,7},{8,9},{9,10},{10,11},{11... | collective-permute-start | bytes 122888 | tf_op jit(solution)/shard_map/ppermute | solution.py:19
  72.0 4.5 %collective-permute-start.12 = (f32[1,32,1024]{2,1,0:T(8,128)S(1)}, f32[1,32,1024]{2,1,0:T(8,128)S(1)}, u32[]{:S(2)}, u32[]{:S(2)}) collective-permute-start(f32[1,32,1024]{2,1,0:T(8,128)S(1)} %get-tuple-element.60), channel_id=1, source_target_pairs={{8,0},{16,8},{24,16},{9,1},{17,9},{25,17},{10,2},{18,10},{26,18},{... | collective-permute-start | bytes 393224 | tf_op jit(solution)/shard_map/ppermute | solution.py:22
  73.7 6.6 %collective-permute-start.13 = (f32[1,32,1024]{2,1,0:T(8,128)S(1)}, f32[1,32,1024]{2,1,0:T(8,128)S(1)}, u32[]{:S(2)}, u32[]{:S(2)}) collective-permute-start(f32[1,32,1024]{2,1,0:T(8,128)S(1)} %get-tuple-element.59), channel_id=1, source_target_pairs={{0,8},{8,16},{16,24},{1,9},{9,17},{17,25},{2,10},{10,18},{18,26},{... | collective-permute-start | bytes 393224 | tf_op jit(solution)/shard_map/ppermute | solution.py:19
  75.6 40.6 %copy-start.3 = (f32[8,32,1023]{2,1,0:T(8,128)}, f32[8,32,1023]{2,1,0:T(8,128)S(1)}, u32[]{:S(2)}) copy-start(f32[8,32,1023]{2,1,0:T(8,128)S(1)} %get-tuple-element.14) | copy-start | bytes 3142660
  80.4 7.7 %collective-permute-start.15 = (f32[10,1,1024]{2,1,0:T(1,128)S(1)}, f32[10,1,1024]{2,1,0:T(1,128)S(1)}, u32[]{:S(2)}, u32[]{:S(2)}) collective-permute-start(f32[10,1,1024]{2,1,0:T(1,128)S(1)} %get-tuple-element.40), channel_id=1, source_target_pairs={{0,1},{1,2},{2,3},{3,4},{4,5},{5,6},{6,7},{8,9},{9,10},{10,11},{11... | collective-permute-start | bytes 122888 | tf_op jit(solution)/shard_map/ppermute | solution.py:19
  85.7 6.2 %collective-permute-start.14 = (f32[10,1,1024]{2,1,0:T(1,128)S(1)}, f32[10,1,1024]{2,1,0:T(1,128)S(1)}, u32[]{:S(2)}, u32[]{:S(2)}) collective-permute-start(f32[10,1,1024]{2,1,0:T(1,128)S(1)} %get-tuple-element.39), channel_id=1, source_target_pairs={{1,0},{2,1},{3,2},{4,3},{5,4},{6,5},{7,6},{9,8},{10,9},{11,10},{12... | collective-permute-start | bytes 122888 | tf_op jit(solution)/shard_map/ppermute | solution.py:22
  88.1 37.9 %copy-start.1 = (f32[9,32,1024]{2,1,0:T(8,128)}, f32[9,32,1024]{2,1,0:T(8,128)S(1)}, u32[]{:S(2)}) copy-start(f32[9,32,1024]{2,1,0:T(8,128)S(1)} %get-tuple-element.16) | copy-start | bytes 3538948
  93.3 5.2 %collective-permute-start.16 = (f32[1,32,1024]{2,1,0:T(8,128)S(1)}, f32[1,32,1024]{2,1,0:T(8,128)S(1)}, u32[]{:S(2)}, u32[]{:S(2)}) collective-permute-start(f32[1,32,1024]{2,1,0:T(8,128)S(1)} %get-tuple-element.58), channel_id=1, source_target_pairs={{8,0},{16,8},{24,16},{9,1},{17,9},{25,17},{10,2},{18,10},{26,18},{... | collective-permute-start | bytes 393224 | tf_op jit(solution)/shard_map/ppermute | solution.py:22
  96.6 5.7 %collective-permute-start.17 = (f32[1,32,1024]{2,1,0:T(8,128)S(1)}, f32[1,32,1024]{2,1,0:T(8,128)S(1)}, u32[]{:S(2)}, u32[]{:S(2)}) collective-permute-start(f32[1,32,1024]{2,1,0:T(8,128)S(1)} %get-tuple-element.57), channel_id=1, source_target_pairs={{0,8},{8,16},{16,24},{1,9},{9,17},{17,25},{2,10},{10,18},{18,26},{... | collective-permute-start | bytes 393224 | tf_op jit(solution)/shard_map/ppermute | solution.py:19
  102.3 5.7 %collective-permute-start.19 = (f32[10,1,1024]{2,1,0:T(1,128)S(1)}, f32[10,1,1024]{2,1,0:T(1,128)S(1)}, u32[]{:S(2)}, u32[]{:S(2)}) collective-permute-start(f32[10,1,1024]{2,1,0:T(1,128)S(1)} %get-tuple-element.38), channel_id=1, source_target_pairs={{0,1},{1,2},{2,3},{3,4},{4,5},{5,6},{6,7},{8,9},{9,10},{10,11},{11... | collective-permute-start | bytes 122888 | tf_op jit(solution)/shard_map/ppermute | solution.py:19
  105.7 6.2 %collective-permute-start.18 = (f32[10,1,1024]{2,1,0:T(1,128)S(1)}, f32[10,1,1024]{2,1,0:T(1,128)S(1)}, u32[]{:S(2)}, u32[]{:S(2)}) collective-permute-start(f32[10,1,1024]{2,1,0:T(1,128)S(1)} %get-tuple-element.37), channel_id=1, source_target_pairs={{1,0},{2,1},{3,2},{4,3},{5,4},{6,5},{7,6},{9,8},{10,9},{11,10},{12... | collective-permute-start | bytes 122888 | tf_op jit(solution)/shard_map/ppermute | solution.py:22
  113.3 3.6 %collective-permute-start.20 = (f32[1,32,1024]{2,1,0:T(8,128)S(1)}, f32[1,32,1024]{2,1,0:T(8,128)S(1)}, u32[]{:S(2)}, u32[]{:S(2)}) collective-permute-start(f32[1,32,1024]{2,1,0:T(8,128)S(1)} %get-tuple-element.56), channel_id=1, source_target_pairs={{8,0},{16,8},{24,16},{9,1},{17,9},{25,17},{10,2},{18,10},{26,18},{... | collective-permute-start | bytes 393224 | tf_op jit(solution)/shard_map/ppermute | solution.py:22
  115.0 5.7 %collective-permute-start.21 = (f32[1,32,1024]{2,1,0:T(8,128)S(1)}, f32[1,32,1024]{2,1,0:T(8,128)S(1)}, u32[]{:S(2)}, u32[]{:S(2)}) collective-permute-start(f32[1,32,1024]{2,1,0:T(8,128)S(1)} %get-tuple-element.55), channel_id=1, source_target_pairs={{0,8},{8,16},{16,24},{1,9},{9,17},{17,25},{2,10},{10,18},{18,26},{... | collective-permute-start | bytes 393224 | tf_op jit(solution)/shard_map/ppermute | solution.py:19
  120.7 5.6 %collective-permute-start.23 = (f32[10,1,1024]{2,1,0:T(1,128)S(1)}, f32[10,1,1024]{2,1,0:T(1,128)S(1)}, u32[]{:S(2)}, u32[]{:S(2)}) collective-permute-start(f32[10,1,1024]{2,1,0:T(1,128)S(1)} %get-tuple-element.36), channel_id=1, source_target_pairs={{0,1},{1,2},{2,3},{3,4},{4,5},{5,6},{6,7},{8,9},{9,10},{10,11},{11... | collective-permute-start | bytes 122888 | tf_op jit(solution)/shard_map/ppermute | solution.py:19
  124.1 6.2 %collective-permute-start.22 = (f32[10,1,1024]{2,1,0:T(1,128)S(1)}, f32[10,1,1024]{2,1,0:T(1,128)S(1)}, u32[]{:S(2)}, u32[]{:S(2)}) collective-permute-start(f32[10,1,1024]{2,1,0:T(1,128)S(1)} %get-tuple-element.35), channel_id=1, source_target_pairs={{1,0},{2,1},{3,2},{4,3},{5,4},{6,5},{7,6},{9,8},{10,9},{11,10},{12... | collective-permute-start | bytes 122888 | tf_op jit(solution)/shard_map/ppermute | solution.py:22
  132.0 41.4 %copy-start.18 = (f32[4,1024]{1,0:T(4,128)S(1)}, f32[4,1024]{1,0:T(4,128)}, u32[]{:S(2)}) copy-start(f32[4,1024]{1,0:T(4,128)} %param.12) | copy-start | bytes 49156
  178.4 7.4 %all-to-all-start.1 = ((f32[32,1,64]{2,1,0:T(1,128)}), f32[32,1,64]{2,1,0:T(1,128)S(1)}, u32[]{:S(2)}, u32[]{:S(2)}) async-start(f32[32,1,64]{2,1,0:T(1,128)} %all_to_all.22), calls=%async_computation.1 | async-start | bytes 32768 | tf_op jit(solution)/shard_map/all_to_all | solution.py:172
  189.9 9.6 %all-to-all-start.2 = ((f32[32,1,64]{2,1,0:T(1,128)}), f32[32,1,64]{2,1,0:T(1,128)S(1)}, u32[]{:S(2)}, u32[]{:S(2)}) async-start(f32[32,1,64]{2,1,0:T(1,128)} %convolution_bitcast_fusion), calls=%async_computation.2 | async-start | bytes 32768 | tf_op jit(solution)/shard_map/all_to_all | solution.py:181
  231.4 5.5 %collective-permute-start.24 = (f32[1,32,1024]{2,1,0:T(8,128)S(1)}, f32[1,32,1024]{2,1,0:T(8,128)S(1)}, u32[]{:S(2)}, u32[]{:S(2)}) collective-permute-start(f32[1,32,1024]{2,1,0:T(8,128)S(1)} %get-tuple-element.54), channel_id=1, source_target_pairs={{8,0},{16,8},{24,16},{9,1},{17,9},{25,17},{10,2},{18,10},{26,18},{... | collective-permute-start | bytes 393224 | tf_op jit(solution)/shard_map/ppermute | solution.py:22
  234.7 5.7 %collective-permute-start.25 = (f32[1,32,1024]{2,1,0:T(8,128)S(1)}, f32[1,32,1024]{2,1,0:T(8,128)S(1)}, u32[]{:S(2)}, u32[]{:S(2)}) collective-permute-start(f32[1,32,1024]{2,1,0:T(8,128)S(1)} %get-tuple-element.53), channel_id=1, source_target_pairs={{0,8},{8,16},{16,24},{1,9},{9,17},{17,25},{2,10},{10,18},{18,26},{... | collective-permute-start | bytes 393224 | tf_op jit(solution)/shard_map/ppermute | solution.py:19
  240.5 7.2 %collective-permute-start.27 = (f32[10,1,1024]{2,1,0:T(1,128)S(1)}, f32[10,1,1024]{2,1,0:T(1,128)S(1)}, u32[]{:S(2)}, u32[]{:S(2)}) collective-permute-start(f32[10,1,1024]{2,1,0:T(1,128)S(1)} %get-tuple-element.34), channel_id=1, source_target_pairs={{0,1},{1,2},{2,3},{3,4},{4,5},{5,6},{6,7},{8,9},{9,10},{10,11},{11... | collective-permute-start | bytes 122888 | tf_op jit(solution)/shard_map/ppermute | solution.py:19
  245.6 6.2 %collective-permute-start.26 = (f32[10,1,1024]{2,1,0:T(1,128)S(1)}, f32[10,1,1024]{2,1,0:T(1,128)S(1)}, u32[]{:S(2)}, u32[]{:S(2)}) collective-permute-start(f32[10,1,1024]{2,1,0:T(1,128)S(1)} %get-tuple-element.33), channel_id=1, source_target_pairs={{1,0},{2,1},{3,2},{4,3},{5,4},{6,5},{7,6},{9,8},{10,9},{11,10},{12... | collective-permute-start | bytes 122888 | tf_op jit(solution)/shard_map/ppermute | solution.py:22
  253.0 5.0 %collective-permute-start.28 = (f32[1,32,1024]{2,1,0:T(8,128)S(1)}, f32[1,32,1024]{2,1,0:T(8,128)S(1)}, u32[]{:S(2)}, u32[]{:S(2)}) collective-permute-start(f32[1,32,1024]{2,1,0:T(8,128)S(1)} %get-tuple-element.52), channel_id=1, source_target_pairs={{8,0},{16,8},{24,16},{9,1},{17,9},{25,17},{10,2},{18,10},{26,18},{... | collective-permute-start | bytes 393224 | tf_op jit(solution)/shard_map/ppermute | solution.py:22
  256.1 5.9 %collective-permute-start.29 = (f32[1,32,1024]{2,1,0:T(8,128)S(1)}, f32[1,32,1024]{2,1,0:T(8,128)S(1)}, u32[]{:S(2)}, u32[]{:S(2)}) collective-permute-start(f32[1,32,1024]{2,1,0:T(8,128)S(1)} %get-tuple-element.51), channel_id=1, source_target_pairs={{0,8},{8,16},{16,24},{1,9},{9,17},{17,25},{2,10},{10,18},{18,26},{... | collective-permute-start | bytes 393224 | tf_op jit(solution)/shard_map/ppermute | solution.py:19
  262.0 5.6 %collective-permute-start.31 = (f32[10,1,1024]{2,1,0:T(1,128)S(1)}, f32[10,1,1024]{2,1,0:T(1,128)S(1)}, u32[]{:S(2)}, u32[]{:S(2)}) collective-permute-start(f32[10,1,1024]{2,1,0:T(1,128)S(1)} %get-tuple-element.32), channel_id=1, source_target_pairs={{0,1},{1,2},{2,3},{3,4},{4,5},{5,6},{6,7},{8,9},{9,10},{10,11},{11... | collective-permute-start | bytes 122888 | tf_op jit(solution)/shard_map/ppermute | solution.py:19
  265.2 6.2 %collective-permute-start.30 = (f32[10,1,1024]{2,1,0:T(1,128)S(1)}, f32[10,1,1024]{2,1,0:T(1,128)S(1)}, u32[]{:S(2)}, u32[]{:S(2)}) collective-permute-start(f32[10,1,1024]{2,1,0:T(1,128)S(1)} %get-tuple-element.31), channel_id=1, source_target_pairs={{1,0},{2,1},{3,2},{4,3},{5,4},{6,5},{7,6},{9,8},{10,9},{11,10},{12... | collective-permute-start | bytes 122888 | tf_op jit(solution)/shard_map/ppermute | solution.py:22
  272.8 5.0 %collective-permute-start.32 = (f32[1,32,1024]{2,1,0:T(8,128)S(1)}, f32[1,32,1024]{2,1,0:T(8,128)S(1)}, u32[]{:S(2)}, u32[]{:S(2)}) collective-permute-start(f32[1,32,1024]{2,1,0:T(8,128)S(1)} %get-tuple-element.50), channel_id=1, source_target_pairs={{8,0},{16,8},{24,16},{9,1},{17,9},{25,17},{10,2},{18,10},{26,18},{... | collective-permute-start | bytes 393224 | tf_op jit(solution)/shard_map/ppermute | solution.py:22
  275.9 5.7 %collective-permute-start.33 = (f32[1,32,1024]{2,1,0:T(8,128)S(1)}, f32[1,32,1024]{2,1,0:T(8,128)S(1)}, u32[]{:S(2)}, u32[]{:S(2)}) collective-permute-start(f32[1,32,1024]{2,1,0:T(8,128)S(1)} %get-tuple-element.49), channel_id=1, source_target_pairs={{0,8},{8,16},{16,24},{1,9},{9,17},{17,25},{2,10},{10,18},{18,26},{... | collective-permute-start | bytes 393224 | tf_op jit(solution)/shard_map/ppermute | solution.py:19
  281.7 5.6 %collective-permute-start.35 = (f32[10,1,1024]{2,1,0:T(1,128)S(1)}, f32[10,1,1024]{2,1,0:T(1,128)S(1)}, u32[]{:S(2)}, u32[]{:S(2)}) collective-permute-start(f32[10,1,1024]{2,1,0:T(1,128)S(1)} %get-tuple-element.30), channel_id=1, source_target_pairs={{0,1},{1,2},{2,3},{3,4},{4,5},{5,6},{6,7},{8,9},{9,10},{10,11},{11... | collective-permute-start | bytes 122888 | tf_op jit(solution)/shard_map/ppermute | solution.py:19
  285.0 6.2 %collective-permute-start.34 = (f32[10,1,1024]{2,1,0:T(1,128)S(1)}, f32[10,1,1024]{2,1,0:T(1,128)S(1)}, u32[]{:S(2)}, u32[]{:S(2)}) collective-permute-start(f32[10,1,1024]{2,1,0:T(1,128)S(1)} %get-tuple-element.29), channel_id=1, source_target_pairs={{1,0},{2,1},{3,2},{4,3},{5,4},{6,5},{7,6},{9,8},{10,9},{11,10},{12... | collective-permute-start | bytes 122888 | tf_op jit(solution)/shard_map/ppermute | solution.py:22
  292.7 3.9 %collective-permute-start.36 = (f32[1,32,1024]{2,1,0:T(8,128)S(1)}, f32[1,32,1024]{2,1,0:T(8,128)S(1)}, u32[]{:S(2)}, u32[]{:S(2)}) collective-permute-start(f32[1,32,1024]{2,1,0:T(8,128)S(1)} %get-tuple-element.48), channel_id=1, source_target_pairs={{8,0},{16,8},{24,16},{9,1},{17,9},{25,17},{10,2},{18,10},{26,18},{... | collective-permute-start | bytes 393224 | tf_op jit(solution)/shard_map/ppermute | solution.py:22
  294.6 5.7 %collective-permute-start.37 = (f32[1,32,1024]{2,1,0:T(8,128)S(1)}, f32[1,32,1024]{2,1,0:T(8,128)S(1)}, u32[]{:S(2)}, u32[]{:S(2)}) collective-permute-start(f32[1,32,1024]{2,1,0:T(8,128)S(1)} %get-tuple-element.47), channel_id=1, source_target_pairs={{0,8},{8,16},{16,24},{1,9},{9,17},{17,25},{2,10},{10,18},{18,26},{... | collective-permute-start | bytes 393224 | tf_op jit(solution)/shard_map/ppermute | solution.py:19
  300.4 5.7 %collective-permute-start.39 = (f32[10,1,1024]{2,1,0:T(1,128)S(1)}, f32[10,1,1024]{2,1,0:T(1,128)S(1)}, u32[]{:S(2)}, u32[]{:S(2)}) collective-permute-start(f32[10,1,1024]{2,1,0:T(1,128)S(1)} %get-tuple-element.28), channel_id=1, source_target_pairs={{0,1},{1,2},{2,3},{3,4},{4,5},{5,6},{6,7},{8,9},{9,10},{10,11},{11... | collective-permute-start | bytes 122888 | tf_op jit(solution)/shard_map/ppermute | solution.py:19
  303.7 6.4 %collective-permute-start.38 = (f32[10,1,1024]{2,1,0:T(1,128)S(1)}, f32[10,1,1024]{2,1,0:T(1,128)S(1)}, u32[]{:S(2)}, u32[]{:S(2)}) collective-permute-start(f32[10,1,1024]{2,1,0:T(1,128)S(1)} %get-tuple-element.27), channel_id=1, source_target_pairs={{1,0},{2,1},{3,2},{4,3},{5,4},{6,5},{7,6},{9,8},{10,9},{11,10},{12... | collective-permute-start | bytes 122888 | tf_op jit(solution)/shard_map/ppermute | solution.py:22
  (14 other events, 130.5 us)
where the time goes:
time: 314 us; the launch traced here: 312 us
  starting transfers between devices  120 us (38%)
  local copies, waits for them, and re-layouts  71.5 us (23%)
  waiting for transfers between devices  59 us (19%)
  other arithmetic  56.5 us (18%)
  matrix products  4.05 us (1%)
    ppermute x20, starting transfers between devices, padded_2(): lax.ppermute(lax.slice_in_dim(block, 0, width, axis=dim), axis, backward)  52.9 us
    ppermute x20, starting transfers between devices, padded_2(): lax.ppermute(lax.slice_in_dim(block, block.shape[dim] - width, None, axis...  49.1 us
    gather x2, local copies, waits for them, and re-layouts, body(): values = jnp.sum(probe_weights * flat[probe_nodes], axis=0)  41.4 us
    ppermute x20, waiting for transfers between devices, padded_2(): lax.ppermute(lax.slice_in_dim(block, 0, width, axis=dim), axis, backward)  29.2 us
    ppermute x20, waiting for transfers between devices, padded_2(): lax.ppermute(lax.slice_in_dim(block, block.shape[dim] - width, None, axis...  26.5 us
    scatter-add x1, other arithmetic, body(): source = jnp.zeros(flat.shape, jnp.float32).at[probe_nodes.reshape(-1)].a...  22.9 us
    another operation x3, other arithmetic  9.14 us
    all_to_all x1, starting transfers between devices, body(): lax.all_to_all(reply, ('px', 'py'), split_axis=0, concat_axis=0, tiled=True)  6.86 us
  transfers between devices with their start and end apart: 43, of which 22 were waited for; matrix products, arithmetic and copies ran while one was open for 23% of the time, Pallas kernels for 0%

commit v1 on v0

v1 whole, which is shorter than its diff:
```python
import functools

import jax
import jax.numpy as jnp
from jax import lax
from jax.experimental import pallas as pl
from jax.experimental.pallas import tpu as pltpu
from jax.sharding import PartitionSpec as P

SWEEPS = 4
STRIP = 8
MESH = pl.DeviceIdType.MESH

bound_low = 1.0
bound_high = 25.0

PERT, BACK, PERMIT, TAN, ADJ = 0, 1, 2, 3, 6
EXCHANGES = 10
SEARCHES = (TAN, ADJ)


def cheb_steps():
    centre = 0.5 * (bound_high + bound_low)
    half_width = 0.5 * (bound_high - bound_low)
    spread = centre / half_width
    ratio = 1.0 / spread
    steps = []
    for _ in range(SWEEPS - 1):
        following = 1.0 / (2.0 * spread - ratio)
        steps.append((following * ratio, 2.0 * following / half_width))
        ratio = following
    return centre, steps


def split_rows(row):
    high = row.astype(jnp.bfloat16).astype(jnp.float32)
    rest = row - high
    middle = rest.astype(jnp.bfloat16).astype(jnp.float32)
    low = rest - middle
    index = lax.broadcasted_iota(jnp.int32, (16, row.shape[1]), 0)
    parts = jnp.where(index == 0, high, jnp.where(index == 1, middle, jnp.where(index == 2, low, 0.0)))
    return parts.astype(jnp.bfloat16)


def kernel(
    n_px, n_py,
    back, pert, permit, nodes, weights, owner, sensor, sensor_weight,
    out,
    search, remain, coef_x, coef_yd, coef_yu, coef_zd, coef_zu, diag,
    halo_x, halo_y, pack_y,
    field_t, row_hot, row_val, z_hot, key_hot, values, sums_py, sums_px,
    send_sem, recv_sem, py_send, py_recv, px_send, px_recv,
):
    rows, cols, depth = back.shape
    strips = cols // STRIP
    last = rows - 1
    probes = nodes.shape[1]
    kinds = nodes.shape[0]
    sensors_dev = sensor_weight.shape[0]
    sensors = key_hot.shape[0]
    nodes_dev = rows * cols
    shift = depth.bit_length() - 1
    assert depth == 1 << shift
    px, py = lax.axis_index("px"), lax.axis_index("py")
    centre, steps = cheb_steps()

    lane = lax.broadcasted_iota(jnp.int32, (STRIP, depth), 1)
    sub = lax.broadcasted_iota(jnp.int32, (STRIP, depth), 0)
    first_lane, last_lane = lane == 0, lane == depth - 1
    first_sub, last_sub = sub == 0, sub == STRIP - 1

    halo_x[...] = jnp.zeros_like(halo_x)
    halo_y[...] = jnp.zeros_like(halo_y)
    for side, face in ((0, 0), (1, last)):
        halo_x[BACK, side] = back[face]
        halo_x[PERMIT, side] = -permit[face]
    for slot, array in ((BACK, back), (PERT, pert), (PERMIT, permit)):
        for x in range(rows):
            for side, face in ((0, 0), (1, cols - 1)):
                row = array[x, face : face + 1, :]
                pack_y[slot, side, x : x + 1, :] = row
                if slot == BACK:
                    halo_y[slot, side, x : x + 1, :] = row
                if slot == PERMIT:
                    halo_y[slot, side, x : x + 1, :] = -row

    barrier = pltpu.get_barrier_semaphore()
    for step in range(1, n_px):
        pl.semaphore_signal(barrier, inc=1, device_id={"px": lax.rem(px + step, n_px)}, device_id_type=MESH)
    for step in range(1, n_py):
        pl.semaphore_signal(barrier, inc=1, device_id={"py": lax.rem(py + step, n_py)}, device_id_type=MESH)
    pl.semaphore_wait(barrier, n_px + n_py - 2)

    def copy(slot, way, array):
        side = way % 2
        if way < 2:
            source = array.at[last if side else 0]
            target = halo_x.at[slot, 1 - side]
            device = {"px": lax.rem(px + (1 if side else n_px - 1), n_px)}
        else:
            source = pack_y.at[slot, side]
            target = halo_y.at[slot, 1 - side]
            device = {"py": lax.rem(py + (1 if side else n_py - 1), n_py)}
        return pltpu.make_async_remote_copy(
            src_ref=source, dst_ref=target, send_sem=send_sem.at[slot, way], recv_sem=recv_sem.at[slot, way],
            device_id=device, device_id_type=MESH,
        )

    sends = (px > 0, px < n_px - 1, py > 0, py < n_py - 1)
    takes = (sends[1], sends[0], sends[3], sends[2])

    def start(slot, way, array):
        @pl.when(sends[way])
        def _():
            copy(slot, way, array).start()

    def finish(slot, ways, array):
        for way in ways:
            @pl.when(takes[way])
            def _():
                copy(slot, way, array).wait_recv()

            @pl.when(sends[way])
            def _():
                copy(slot, way, array).wait_send()

    for slot, array in ((PERT, pert), (BACK, back), (PERMIT, permit)):
        for way in (2, 3, 0, 1):
            start(slot, way, array)

    def hots(kind, _):
        node = nodes[pl.ds(kind, 1), :]
        at_row = lax.shift_right_logical(node, shift)
        at_depth = lax.bitwise_and(node, depth - 1)
        columns = pl.ds(pl.multiple_of(kind * probes, probes), probes)
        index = lax.broadcasted_iota(jnp.int32, (16, probes), 0)

        def row_block(block, _):
            first = pl.multiple_of(block * 16, 16)
            row_hot[pl.ds(first, 16), columns] = jnp.where(index + first == at_row, 1.0, 0.0).astype(jnp.bfloat16)
            return 0

        def z_block(block, _):
            first = pl.multiple_of(block * 16, 16)
            z_hot[pl.ds(first, 16), columns] = jnp.where(index + first == at_depth, 1.0, 0.0).astype(jnp.bfloat16)
            return 0

        lax.fori_loop(0, nodes_dev // 16, row_block, 0)
        lax.fori_loop(0, depth // 16, z_block, 0)
        return 0

    lax.fori_loop(0, kinds, hots, 0)
    key = owner[...] * sensors_dev + sensor[...]
    key_index = lax.broadcasted_iota(jnp.int32, (16, probes), 0)

    def key_block(block, _):
        first = pl.multiple_of(block * 16, 16)
        key_hot[pl.ds(first, 16), :] = jnp.where(key_index + first == key, 1.0, 0.0).astype(jnp.bfloat16)
        return 0

    lax.fori_loop(0, sensors // 16, key_block, 0)

    def around(array, below, above, slot, x, strip):
        y = strip * STRIP
        here = array[x, y : y + STRIP, :]
        xd, xu = below[y : y + STRIP, :], above[y : y + STRIP, :]
        before = array[x, y - 1 : y, :] if strip > 0 else halo_y[slot, 0, pl.ds(x, 1), :]
        after = array[x, y + STRIP : y + STRIP + 1, :] if strip < strips - 1 else halo_y[slot, 1, pl.ds(x, 1), :]
        yd = jnp.where(first_sub, before, pltpu.roll(here, 1, 0))
        yu = jnp.where(last_sub, after, pltpu.roll(here, STRIP - 1, 0))
        zd, zu = pltpu.roll(here, 1, 1), pltpu.roll(here, depth - 1, 1)
        return here, (xd, xu, yd, yu, zd, zu)

    def planes(plane, slots, arrays, after_face):
        for slot, array in zip(slots, arrays):
            finish(slot, (2, 3), array)

        def inner(x, _):
            plane(x, [a.at[x - 1] for a in arrays], [a.at[x + 1] for a in arrays])
            return 0

        lax.fori_loop(1, last, inner, 0)
        for slot, array in zip(slots, arrays):
            finish(slot, (0, 1), array)
        plane(0, [halo_x.at[s, 0] for s in slots], [a.at[1] for a in arrays])
        after_face(0)
        plane(last, [a.at[last - 1] for a in arrays], [halo_x.at[s, 1] for s in slots])
        after_face(1)

    def send_y(slot, array):
        for x in range(rows):
            for side, face in ((0, 0), (1, cols - 1)):
                pack_y[slot, side, x : x + 1, :] = array[x, face : face + 1, :]
        start(slot, 2, array)
        start(slot, 3, array)

    def source_plane(x, below, above):
        for strip in range(strips):
            y = strip * STRIP
            c, c_near = around(pert, below[0], above[0], PERT, x, strip)
            f, f_near = around(back, below[1], above[1], BACK, x, strip)
            terms = [(c + cn) * (fn - f) for cn, fn in zip(c_near, f_near)]
            total = terms[0] + terms[1] + terms[2] + terms[3]
            total = total + jnp.where(first_lane, 0.0, terms[4]) + jnp.where(last_lane, 0.0, terms[5])
            total = 0.5 * total
            remain[x, y : y + STRIP, :] = total
            search[0, x, y : y + STRIP, :] = total / centre

    planes(source_plane, (PERT, BACK), (pert, back), lambda side: start(TAN, side, search.at[0]))
    send_y(TAN, search.at[0])

    def coef_plane(x, below, above):
        for strip in range(strips):
            y = strip * STRIP
            c, (xd, xu, yd, yu, zd, zu) = around(permit, below[0], above[0], PERMIT, x, strip)
            xd, xu, yd, yu = 0.5 * (c + xd), 0.5 * (c + xu), 0.5 * (c + yd), 0.5 * (c + yu)
            zd = jnp.where(first_lane, 0.0, 0.5 * (c + zd))
            zu = jnp.where(last_lane, 0.0, 0.5 * (c + zu))
            coef_x[x, y : y + STRIP, :] = xd
            if isinstance(x, int) and x == last:
                coef_x[rows, y : y + STRIP, :] = xu
            coef_yd[x, y : y + STRIP, :] = yd
            coef_yu[x, y : y + STRIP, :] = yu
            coef_zd[x, y : y + STRIP, :] = zd
            coef_zu[x, y : y + STRIP, :] = zu
            diag[x, y : y + STRIP, :] = 1.0 + ((xd + xu) + (yd + yu) + (zd + zu))

    planes(coef_plane, (PERMIT,), (permit,), lambda side: None)

    def solve(first):
        for sweep, (keep, gain) in enumerate(steps):
            slot = first + sweep
            now, later = search.at[sweep], search.at[sweep + 1]
            sent = sweep < SWEEPS - 2 or first == ADJ

            def sweep_plane(x, below, above):
                for strip in range(strips):
                    y = strip * STRIP
                    at = (x, slice(y, y + STRIP))
                    f, (xd, xu, yd, yu, zd, zu) = around(now, below[0], above[0], slot, x, strip)
                    off = coef_x[at] * xd + coef_x[x + 1, y : y + STRIP, :] * xu
                    off = off + (coef_yd[at] * yd + coef_yu[at] * yu)
                    off = off + (coef_zd[at] * zd + coef_zu[at] * zu)
                    left = remain[at] - diag[at] * f + off
                    remain[at] = left
                    later[at] = keep * f + gain * left

            def after_face(side):
                if sent:
                    start(slot + 1, side, later)

            planes(sweep_plane, (slot,), (now,), after_face)
            if sent:
                send_y(slot + 1, later)

        def total_plane(x, _):
            for strip in range(strips):
                at = (x, slice(strip * STRIP, (strip + 1) * STRIP))
                total = search[(0,) + at]
                for index in range(1, SWEEPS):
                    total = total + search[(index,) + at]
                remain[at] = total
            return 0

        lax.fori_loop(0, rows, total_plane, 0)

    solve(TAN)

    for x in range(rows):
        turned = remain[x].T
        high = turned.astype(jnp.bfloat16)
        field_t[:, x * cols : (x + 1) * cols] = high
        field_t[:, nodes_dev + x * cols : nodes_dev + (x + 1) * cols] = (turned - high.astype(jnp.float32)).astype(jnp.bfloat16)

    width = probes // 2
    tall = 256
    values[...] = jnp.zeros_like(values)

    def pick(kind, _):
        for half in range(2):
            spot = pl.ds(half * width, width)
            columns = pl.ds(pl.multiple_of(kind * probes + half * width, width), width)
            at_depth = lax.bitwise_and(nodes[pl.ds(kind, 1), spot], depth - 1)
            hot = row_hot[:, columns]
            hot = jnp.concatenate([hot, hot], axis=0)
            index = lax.broadcasted_iota(jnp.int32, (tall, width), 0)
            found = jnp.zeros((1, width), jnp.float32)
            for block in range(depth // tall):
                lines = jnp.dot(field_t[block * tall : (block + 1) * tall, :], hot, preferred_element_type=jnp.float32)
                found = found + jnp.sum(jnp.where(index + block * tall == at_depth, lines, 0.0), axis=0, keepdims=True)
            values[:, spot] += weights[pl.ds(kind, 1), spot] * found
        return 0

    lax.fori_loop(0, kinds, pick, 0)

    contract_lanes = (((1,), (1,)), ((), ()))
    partial = lax.dot_general(split_rows(values[...]), key_hot[...], contract_lanes, preferred_element_type=jnp.float32)
    partial = jnp.sum(partial, axis=0, keepdims=True)
    place = lax.broadcasted_iota(jnp.int32, (1, sensors), 1) - (px * n_py + py) * sensors_dev
    own = jnp.zeros((1, sensors), jnp.float32)
    for index in range(sensors_dev):
        own = jnp.where(place == index, sensor_weight[index], own)
    line = lax.broadcasted_iota(jnp.int32, (8, sensors), 0)
    sums_py[0] = jnp.where(line == 0, partial, jnp.where(line == 1, own, 0.0))

    def all_sum(sums, count, me, axis, sent, got):
        copies = []
        for step in range(1, count):
            move = pltpu.make_async_remote_copy(
                src_ref=sums.at[0], dst_ref=sums.at[step], send_sem=sent.at[step], recv_sem=got.at[step],
                device_id={axis: lax.rem(me + step, count)}, device_id_type=MESH,
            )
            move.start()
            copies.append(move)
        total = sums[0]
        for step, move in enumerate(copies):
            move.wait()
            total = total + sums[step + 1]
        return total

    sums_px[0] = all_sum(sums_py, n_py, py, "py", py_send, py_recv)
    total = all_sum(sums_px, n_px, px, "px", px_send, px_recv)
    weighted = total[0:1] * total[1:2]
    returned = jnp.dot(split_rows(weighted), key_hot[...], preferred_element_type=jnp.float32)
    returned = jnp.sum(returned, axis=0, keepdims=True)

    for kind in range(kinds):
        columns = slice(kind * probes, (kind + 1) * probes)
        value = weights[kind : kind + 1, :] * returned
        high = value.astype(jnp.bfloat16)
        low = (value - high.astype(jnp.float32)).astype(jnp.bfloat16)
        row_val[0:nodes_dev, columns] = row_hot[:, columns] * high
        row_val[nodes_dev:, columns] = row_hot[:, columns] * low

    for block in range(depth // tall):
        span = slice(block * tall, (block + 1) * tall)
        both = lax.dot_general(row_val[...], z_hot[span, :], contract_lanes, preferred_element_type=jnp.float32)
        both = (both[:nodes_dev] + both[nodes_dev:]).reshape(rows, cols, tall)
        remain[:, :, span] = both
        search[0, :, :, span] = both / centre
    start(ADJ, 0, search.at[0])
    start(ADJ, 1, search.at[0])
    send_y(ADJ, search.at[0])

    solve(ADJ)

    end = ADJ + SWEEPS - 1

    def sum_halo(halo, side):
        halo[end, side] = (halo[ADJ, side] + halo[ADJ + 1, side]) + (halo[ADJ + 2, side] + halo[end, side])

    finish(end, (2, 3), search.at[SWEEPS - 1])
    for side in range(2):
        sum_halo(halo_y, side)

    def sense_plane(x, below, above):
        for strip in range(strips):
            y = strip * STRIP
            b, b_near = around(back, below[0], above[0], BACK, x, strip)
            a, a_near = around(remain, below[1], above[1], end, x, strip)
            terms = [(b - bn) * (a - an) for bn, an in zip(b_near, a_near)]
            total = terms[0] + terms[1] + terms[2] + terms[3]
            total = total + jnp.where(first_lane, 0.0, terms[4]) + jnp.where(last_lane, 0.0, terms[5])
            out[x, y : y + STRIP, :] = -0.5 * total

    def inner(x, _):
        sense_plane(x, [back.at[x - 1], remain.at[x - 1]], [back.at[x + 1], remain.at[x + 1]])
        return 0

    lax.fori_loop(1, last, inner, 0)
    finish(end, (0, 1), search.at[SWEEPS - 1])
    for side in range(2):
        sum_halo(halo_x, side)
    sense_plane(0, [halo_x.at[BACK, 0], halo_x.at[end, 0]], [back.at[1], remain.at[1]])
    sense_plane(last, [back.at[last - 1], remain.at[last - 1]], [halo_x.at[BACK, 1], halo_x.at[end, 1]])


def body(back, pert, permit, nodes, weights, owner, sensor, sensor_weight):
    n_px, n_py = lax.axis_size("px"), lax.axis_size("py")
    rows, cols, depth = back.shape
    kinds, probes = nodes.shape
    sensors = sensor_weight.shape[0] * n_px * n_py
    nodes_dev = rows * cols
    f32, bf16 = jnp.float32, jnp.bfloat16
    vmem = pl.BlockSpec(memory_space=pltpu.VMEM)
    smem = pl.BlockSpec(memory_space=pltpu.SMEM)
    block = pltpu.VMEM((rows, cols, depth), f32)
    dma = pltpu.SemaphoreType.DMA
    return pl.pallas_call(
        functools.partial(kernel, n_px, n_py),
        out_shape=jax.ShapeDtypeStruct((rows, cols, depth), f32),
        in_specs=[vmem] * 7 + [smem],
        out_specs=vmem,
        scratch_shapes=[
            pltpu.VMEM((SWEEPS, rows, cols, depth), f32),
            block,
            pltpu.VMEM((rows + 1, cols, depth), f32),
            block, block, block, block, block,
            pltpu.VMEM((EXCHANGES, 2, cols, depth), f32),
            pltpu.VMEM((EXCHANGES, 2, rows, depth), f32),
            pltpu.VMEM((EXCHANGES, 2, rows, depth), f32),
            pltpu.VMEM((depth, 2 * nodes_dev), bf16),
            pltpu.VMEM((nodes_dev, kinds * probes), bf16),
            pltpu.VMEM((2 * nodes_dev, kinds * probes), bf16),
            pltpu.VMEM((depth, kinds * probes), bf16),
            pltpu.VMEM((sensors, probes), bf16),
            pltpu.VMEM((1, probes), f32),
            pltpu.VMEM((n_py, 8, sensors), f32),
            pltpu.VMEM((n_px, 8, sensors), f32),
            dma((EXCHANGES, 4)), dma((EXCHANGES, 4)),
            dma((n_py,)), dma((n_py,)), dma((n_px,)), dma((n_px,)),
        ],
        compiler_params=pltpu.CompilerParams(
            collective_id=0, has_side_effects=True, vmem_limit_bytes=56 * 1024 * 1024
        ),
        cost_estimate=pl.CostEstimate(flops=10_000_000_000, bytes_accessed=4_500_000, transcendentals=0),
    )(
        back, pert, permit, nodes, weights, owner.reshape(1, probes), sensor.reshape(1, probes), sensor_weight
    )


def solution(mesh):
    placed = (
        P("px", "py", None),
        P("px", "py", None),
        P("px", "py", None),
        P(None, ("px", "py")),
        P(None, ("px", "py")),
        P(("px", "py"), None),
        P(("px", "py")),
        P(("px", "py")),
    )
    return jax.shard_map(
        body, mesh=mesh, in_specs=placed, out_specs=P("px", "py", None), check_vma=False
    )
```

time: 314 us -> 73.1 us (0.23)
  the two profiles are of different devices: /device:TPU:27 before, /device:TPU:0 now
where the time goes in v1:
time: 73.1 us; the launch traced here: 72.9 us
  Pallas kernels  70.6 us (97%)
  local copies, waits for them, and re-layouts  2.31 us (3%)
    pallas_call x1, Pallas kernels, body(): pl.pallas_call(functools.partial(kernel, n_px, n_py), out_shape=jax.Shape...  70.6 us
    unnamed x1, local copies, waits for them, and re-layouts  2.31 us

profile of v1, /device:TPU:0, one launch (start us, length us, event | category | flops | bytes accessed | tf_op | source)
XLA Modules:
  0.0 72.9 jit_solution(7910155682622671288)
XLA Ops:
  0.0 70.6 %shard_map.82 = f32[8,32,1024]{2,1,0:T(8,128)} custom-call(f32[8,32,1024]{2,1,0:T(8,128)} %back.1, f32[8,32,1024]{2,1,0:T(8,128)} %pert.1, f32[8,32,1024]{2,1,0:T(8,128)} %permit.1, s32[4,1024]{1,0:T(4,128)} %nodes.1, f32[4,1024]{1,0:T(4,128)} %weights.1, s32[1,1024]{1,0:T(1,128)} %bitcast.2, s32[1,1024]{1,0:T(1,128)} %bitcast.3, f32[8]{0:T(128)} %sensor_weight.1), custom_call_target="tpu_custom_call" | custom-call | flops 10000000000 | bytes 4500000 | tf_op jit(solution)/shard_map/pallas_call | solution.py:389
  70.6 2.3 %copy.10 = f32[8,32,1024]{2,1,0:T(8,128)} copy(f32[8,32,1024]{2,1,0:T(8,128)} %shard_map.82) | data formatting | bytes 2097152

commit v2 on v1

v2 whole, which is shorter than its diff:
```python
import functools

import jax
import jax.numpy as jnp
from jax import lax
from jax.experimental import pallas as pl
from jax.experimental.pallas import tpu as pltpu
from jax.sharding import PartitionSpec as P

SWEEPS = 4
STRIP = 8
MESH = pl.DeviceIdType.MESH

bound_low = 1.0
bound_high = 25.0

PERT, BACK, PERMIT, TAN, ADJ = 0, 1, 2, 3, 6
EXCHANGES = 10


def cheb_steps():
    centre = 0.5 * (bound_high + bound_low)
    half_width = 0.5 * (bound_high - bound_low)
    spread = centre / half_width
    ratio = 1.0 / spread
    steps = []
    for _ in range(SWEEPS - 1):
        following = 1.0 / (2.0 * spread - ratio)
        steps.append((following * ratio, 2.0 * following / half_width))
        ratio = following
    return centre, steps


def split_rows(row):
    high = row.astype(jnp.bfloat16).astype(jnp.float32)
    rest = row - high
    middle = rest.astype(jnp.bfloat16).astype(jnp.float32)
    low = rest - middle
    index = lax.broadcasted_iota(jnp.int32, (16, row.shape[1]), 0)
    parts = jnp.where(index == 0, high, jnp.where(index == 1, middle, jnp.where(index == 2, low, 0.0)))
    return parts.astype(jnp.bfloat16)


def kernel(
    n_px, n_py,
    back, pert, permit, nodes, weights, owner, sensor, sensor_weight,
    out,
    search, remain, coef_x, coef_yd, coef_yu, coef_zd, coef_zu, diag,
    halo_x, halo_y, pack_y,
    field_t, row_hot, row_val, z_hot, key_hot, values, sums_py, sums_px,
    x_send, x_recv, y_send, y_recv, py_send, py_recv, px_send, px_recv,
):
    rows, cols, depth = back.shape
    strips = cols // STRIP
    last = rows - 1
    probes = nodes.shape[1]
    kinds = nodes.shape[0]
    sensors_dev = sensor_weight.shape[0]
    sensors = key_hot.shape[0]
    nodes_dev = rows * cols
    shift = depth.bit_length() - 1
    assert depth == 1 << shift
    px, py = lax.axis_index("px"), lax.axis_index("py")
    centre, steps = cheb_steps()

    lane = lax.broadcasted_iota(jnp.int32, (STRIP, depth), 1)
    sub = lax.broadcasted_iota(jnp.int32, (STRIP, depth), 0)
    first_lane, last_lane = lane == 0, lane == depth - 1
    first_sub, last_sub = sub == 0, sub == STRIP - 1

    halo_x[...] = jnp.zeros_like(halo_x)
    halo_y[...] = jnp.zeros_like(halo_y)
    pack_y[...] = jnp.zeros_like(pack_y)
    for side, face in ((0, 0), (1, last)):
        halo_x[BACK, side] = back[face]
        halo_x[PERMIT, side] = -permit[face]
    for slot, array in ((BACK, back), (PERT, pert), (PERMIT, permit)):
        for x in range(rows):
            for side, face in ((0, 0), (1, cols - 1)):
                row = array[x, face : face + 1, :]
                pack_y[slot, 0, side, x : x + 1, :] = row
                if slot == BACK:
                    halo_y[slot, 0, side, x : x + 1, :] = row
                if slot == PERMIT:
                    halo_y[slot, 0, side, x : x + 1, :] = -row

    barrier = pltpu.get_barrier_semaphore()
    for step in range(1, n_px):
        pl.semaphore_signal(barrier, inc=1, device_id={"px": lax.rem(px + step, n_px)}, device_id_type=MESH)
    for step in range(1, n_py):
        pl.semaphore_signal(barrier, inc=1, device_id={"py": lax.rem(py + step, n_py)}, device_id_type=MESH)
    pl.semaphore_wait(barrier, n_px + n_py - 2)

    def copy_x(slot, side, strip, array):
        span = pl.ds(strip * STRIP, STRIP)
        return pltpu.make_async_remote_copy(
            src_ref=array.at[last if side else 0, span], dst_ref=halo_x.at[slot, 1 - side, span],
            send_sem=x_send.at[slot, side, strip], recv_sem=x_recv.at[slot, side, strip],
            device_id={"px": lax.rem(px + (1 if side else n_px - 1), n_px)}, device_id_type=MESH,
        )

    def copy_y(slot, side, part):
        return pltpu.make_async_remote_copy(
            src_ref=pack_y.at[slot, part, side], dst_ref=halo_y.at[slot, part, 1 - side],
            send_sem=y_send.at[slot, side, part], recv_sem=y_recv.at[slot, side, part],
            device_id={"py": lax.rem(py + (1 if side else n_py - 1), n_py)}, device_id_type=MESH,
        )

    has_x = (px > 0, px < n_px - 1)
    has_y = (py > 0, py < n_py - 1)
    order = (0, strips - 1) + tuple(range(1, strips - 1))

    def start_x(slot, strip, array):
        for side in range(2):
            pl.when(has_x[side])(lambda: copy_x(slot, side, strip, array).start())

    def start_y(slot, side, part):
        pl.when(has_y[side])(lambda: copy_y(slot, side, part).start())

    def take_x(slot, strip, array):
        for side in range(2):
            pl.when(has_x[1 - side])(lambda: copy_x(slot, side, strip, array).wait_recv())

    def take_y(slot, side, part):
        pl.when(has_y[side])(lambda: copy_y(slot, 1 - side, part).wait_recv())

    def sent(slot, parts, array):
        for side in range(2):
            @pl.when(has_x[side])
            def _():
                for strip in range(strips):
                    copy_x(slot, side, strip, array).wait_send()

            @pl.when(has_y[side])
            def _():
                for part in parts:
                    copy_y(slot, side, part).wait_send()

    fields = ((PERT, pert), (BACK, back), (PERMIT, permit))
    for slot, _ in fields:
        for side in range(2):
            start_y(slot, side, 0)
    for strip in order:
        for slot, array in fields[:2]:
            start_x(slot, strip, array)
    for strip in order:
        start_x(PERMIT, strip, permit)

    def hots(kind, _):
        node = nodes[pl.ds(kind, 1), :]
        at_row = lax.shift_right_logical(node, shift)
        at_depth = lax.bitwise_and(node, depth - 1)
        columns = pl.ds(pl.multiple_of(kind * probes, probes), probes)
        index = lax.broadcasted_iota(jnp.int32, (16, probes), 0)

        def row_block(block, _):
            first = pl.multiple_of(block * 16, 16)
            row_hot[pl.ds(first, 16), columns] = jnp.where(index + first == at_row, 1.0, 0.0).astype(jnp.bfloat16)
            return 0

        def z_block(block, _):
            first = pl.multiple_of(block * 16, 16)
            z_hot[pl.ds(first, 16), columns] = jnp.where(index + first == at_depth, 1.0, 0.0).astype(jnp.bfloat16)
            return 0

        lax.fori_loop(0, nodes_dev // 16, row_block, 0)
        lax.fori_loop(0, depth // 16, z_block, 0)
        return 0

    lax.fori_loop(0, kinds, hots, 0)
    key = owner[...] * sensors_dev + sensor[...]
    key_index = lax.broadcasted_iota(jnp.int32, (16, probes), 0)

    def key_block(block, _):
        first = pl.multiple_of(block * 16, 16)
        key_hot[pl.ds(first, 16), :] = jnp.where(key_index + first == key, 1.0, 0.0).astype(jnp.bfloat16)
        return 0

    lax.fori_loop(0, sensors // 16, key_block, 0)

    def around(array, below, above, slot, x, strip):
        y = strip * STRIP
        part = 1 if slot >= TAN and isinstance(x, int) else 0
        here = array[x, y : y + STRIP, :]
        xd, xu = below[y : y + STRIP, :], above[y : y + STRIP, :]
        before = array[x, y - 1 : y, :] if strip > 0 else halo_y[slot, part, 0, pl.ds(x, 1), :]
        after = array[x, y + STRIP : y + STRIP + 1, :] if strip < strips - 1 else halo_y[slot, part, 1, pl.ds(x, 1), :]
        yd = jnp.where(first_sub, before, pltpu.roll(here, 1, 0))
        yu = jnp.where(last_sub, after, pltpu.roll(here, STRIP - 1, 0))
        zd, zu = pltpu.roll(here, 1, 1), pltpu.roll(here, depth - 1, 1)
        return here, (xd, xu, yd, yu, zd, zu)

    def inner_planes(work, slots, arrays):
        for slot in slots:
            take_y(slot, 0, 0)
            take_y(slot, 1, 0)

        def step(x, _):
            for strip in range(strips):
                work(x, strip, [a.at[x - 1] for a in arrays], [a.at[x + 1] for a in arrays])
            return 0

        lax.fori_loop(1, last, step, 0)

    def outer_planes(work, slots, arrays, after):
        for strip in order:
            for slot, array in zip(slots, arrays):
                take_x(slot, strip, array)
                if slot >= TAN:
                    for side, edge in ((0, 0), (1, strips - 1)):
                        if strip == edge:
                            take_y(slot, side, 1)
            work(0, strip, [halo_x.at[s, 0] for s in slots], [a.at[1] for a in arrays])
            work(last, strip, [a.at[last - 1] for a in arrays], [halo_x.at[s, 1] for s in slots])
            after(strip)

    def nothing(strip):
        return None

    def send_inner(slot, array):
        for side, face in ((0, 0), (1, cols - 1)):
            for x in range(1, last):
                pack_y[slot, 0, side, x : x + 1, :] = array[x, face : face + 1, :]
            start_y(slot, side, 0)

    def send_outer(slot, array):
        def after(strip):
            start_x(slot, strip, array)
            for side, edge, face in ((0, 0, 0), (1, strips - 1, cols - 1)):
                if strip == edge:
                    for x in (0, last):
                        pack_y[slot, 1, side, x : x + 1, :] = array[x, face : face + 1, :]
                    start_y(slot, side, 1)

        return after

    def source_work(x, strip, below, above):
        y = strip * STRIP
        c, c_near = around(pert, below[0], above[0], PERT, x, strip)
        f, f_near = around(back, below[1], above[1], BACK, x, strip)
        terms = [(c + cn) * (fn - f) for cn, fn in zip(c_near, f_near)]
        total = terms[0] + terms[1] + terms[2] + terms[3]
        total = total + jnp.where(first_lane, 0.0, terms[4]) + jnp.where(last_lane, 0.0, terms[5])
        total = 0.5 * total
        remain[x, y : y + STRIP, :] = total
        search[0, x, y : y + STRIP, :] = total / centre

    def coef_work(x, strip, below, above):
        y = strip * STRIP
        c, (xd, xu, yd, yu, zd, zu) = around(permit, below[0], above[0], PERMIT, x, strip)
        xd, xu, yd, yu = 0.5 * (c + xd), 0.5 * (c + xu), 0.5 * (c + yd), 0.5 * (c + yu)
        zd = jnp.where(first_lane, 0.0, 0.5 * (c + zd))
        zu = jnp.where(last_lane, 0.0, 0.5 * (c + zu))
        coef_x[x, y : y + STRIP, :] = xd
        if isinstance(x, int) and x == last:
            coef_x[rows, y : y + STRIP, :] = xu
        coef_yd[x, y : y + STRIP, :] = yd
        coef_yu[x, y : y + STRIP, :] = yu
        coef_zd[x, y : y + STRIP, :] = zd
        coef_zu[x, y : y + STRIP, :] = zu
        diag[x, y : y + STRIP, :] = 1.0 + ((xd + xu) + (yd + yu) + (zd + zu))

    inner_planes(source_work, (PERT, BACK), (pert, back))
    send_inner(TAN, search.at[0])
    inner_planes(coef_work, (PERMIT,), (permit,))
    outer_planes(source_work, (PERT, BACK), (pert, back), send_outer(TAN, search.at[0]))
    outer_planes(coef_work, (PERMIT,), (permit,), nothing)
    for slot, array in fields:
        sent(slot, (0,), array)

    def solve(first):
        for sweep, (keep, gain) in enumerate(steps):
            slot = first + sweep
            now, later = search.at[sweep], search.at[sweep + 1]
            more = sweep < SWEEPS - 2 or first == ADJ

            def sweep_work(x, strip, below, above):
                y = strip * STRIP
                at = (x, slice(y, y + STRIP))
                f, (xd, xu, yd, yu, zd, zu) = around(now, below[0], above[0], slot, x, strip)
                off = coef_x[at] * xd + coef_x[x + 1, y : y + STRIP, :] * xu
                off = off + (coef_yd[at] * yd + coef_yu[at] * yu)
                off = off + (coef_zd[at] * zd + coef_zu[at] * zu)
                left = remain[at] - diag[at] * f + off
                remain[at] = left
                later[at] = keep * f + gain * left

            inner_planes(sweep_work, (slot,), (now,))
            if more:
                send_inner(slot + 1, later)
            outer_planes(sweep_work, (slot,), (now,), send_outer(slot + 1, later) if more else nothing)
            sent(slot, (0, 1), now)

        def total_plane(x, _):
            for strip in range(strips):
                at = (x, slice(strip * STRIP, (strip + 1) * STRIP))
                total = search[(0,) + at]
                for index in range(1, SWEEPS):
                    total = total + search[(index,) + at]
                remain[at] = total
            return 0

        lax.fori_loop(0, rows, total_plane, 0)

    solve(TAN)

    group = 128 // cols
    for part in range(rows // group):
        turned = remain[part * group : (part + 1) * group].reshape(128, depth).T
        high = turned.astype(jnp.bfloat16)
        field_t[:, part * 128 : (part + 1) * 128] = high
        field_t[:, nodes_dev + part * 128 : nodes_dev + (part + 1) * 128] = (turned - high.astype(jnp.float32)).astype(jnp.bfloat16)

    width = probes // 2
    tall = 256
    values[...] = jnp.zeros_like(values)
    index = lax.broadcasted_iota(jnp.int32, (depth, width), 0)

    def pick(kind, _):
        for half in range(2):
            spot = pl.ds(half * width, width)
            columns = pl.ds(pl.multiple_of(kind * probes + half * width, width), width)
            at_depth = lax.bitwise_and(nodes[pl.ds(kind, 1), spot], depth - 1)
            hot = row_hot[:, columns]
            hot = jnp.concatenate([hot, hot], axis=0)
            lines = jnp.dot(field_t[...], hot, preferred_element_type=jnp.float32)
            found = jnp.sum(jnp.where(index == at_depth, lines, 0.0), axis=0, keepdims=True)
            values[:, spot] += weights[pl.ds(kind, 1), spot] * found
        return 0

    lax.fori_loop(0, kinds, pick, 0)

    contract_lanes = (((1,), (1,)), ((), ()))
    partial = lax.dot_general(split_rows(values[...]), key_hot[...], contract_lanes, preferred_element_type=jnp.float32)
    partial = jnp.sum(partial, axis=0, keepdims=True)
    place = lax.broadcasted_iota(jnp.int32, (1, sensors), 1) - (px * n_py + py) * sensors_dev
    own = jnp.zeros((1, sensors), jnp.float32)
    for index in range(sensors_dev):
        own = jnp.where(place == index, sensor_weight[index], own)
    line = lax.broadcasted_iota(jnp.int32, (8, sensors), 0)
    sums_py[0] = jnp.where(line == 0, partial, jnp.where(line == 1, own, 0.0))

    def all_sum(sums, count, me, axis, sent, got):
        copies = []
        for step in range(1, count):
            move = pltpu.make_async_remote_copy(
                src_ref=sums.at[0], dst_ref=sums.at[step], send_sem=sent.at[step], recv_sem=got.at[step],
                device_id={axis: lax.rem(me + step, count)}, device_id_type=MESH,
            )
            move.start()
            copies.append(move)
        total = sums[0]
        for step, move in enumerate(copies):
            move.wait()
            total = total + sums[step + 1]
        return total

    sums_px[0] = all_sum(sums_py, n_py, py, "py", py_send, py_recv)
    total = all_sum(sums_px, n_px, px, "px", px_send, px_recv)
    weighted = total[0:1] * total[1:2]
    returned = jnp.dot(split_rows(weighted), key_hot[...], preferred_element_type=jnp.float32)
    returned = jnp.sum(returned, axis=0, keepdims=True)

    for kind in range(kinds):
        columns = slice(kind * probes, (kind + 1) * probes)
        value = weights[kind : kind + 1, :] * returned
        high = value.astype(jnp.bfloat16)
        low = (value - high.astype(jnp.float32)).astype(jnp.bfloat16)
        row_val[0:nodes_dev, columns] = row_hot[:, columns] * high
        row_val[nodes_dev:, columns] = row_hot[:, columns] * low

    for block in range(depth // tall):
        span = slice(block * tall, (block + 1) * tall)
        both = lax.dot_general(row_val[...], z_hot[span, :], contract_lanes, preferred_element_type=jnp.float32)
        both = (both[:nodes_dev] + both[nodes_dev:]).reshape(rows, cols, tall)
        remain[:, :, span] = both
        search[0, :, :, span] = both / centre
    for strip in order:
        send_outer(ADJ, search.at[0])(strip)
    send_inner(ADJ, search.at[0])

    solve(ADJ)

    end = ADJ + SWEEPS - 1

    def sum_halo(halo, at):
        halo[(end,) + at] = (halo[(ADJ,) + at] + halo[(ADJ + 1,) + at]) + (halo[(ADJ + 2,) + at] + halo[(end,) + at])

    def sense_work(x, strip, below, above):
        y = strip * STRIP
        b, b_near = around(back, below[0], above[0], BACK, x, strip)
        a, a_near = around(remain, below[1], above[1], end, x, strip)
        terms = [(b - bn) * (a - an) for bn, an in zip(b_near, a_near)]
        total = terms[0] + terms[1] + terms[2] + terms[3]
        total = total + jnp.where(first_lane, 0.0, terms[4]) + jnp.where(last_lane, 0.0, terms[5])
        out[x, y : y + STRIP, :] = total

    def sum_strip(strip):
        for side, edge in ((0, 0), (1, strips - 1)):
            sum_halo(halo_x, (side, slice(strip * STRIP, (strip + 1) * STRIP)))
            if strip == edge:
                sum_halo(halo_y, (1, side))

    newest = search.at[SWEEPS - 1]
    for side in range(2):
        take_y(end, side, 0)
        sum_halo(halo_y, (0, side))
    inner_planes(sense_work, (), (back, remain))
    for strip in order:
        take_x(end, strip, newest)
        for side, edge in ((0, 0), (1, strips - 1)):
            if strip == edge:
                take_y(end, side, 1)
        sum_strip(strip)
        sense_work(0, strip, [halo_x.at[BACK, 0], halo_x.at[end, 0]], [back.at[1], remain.at[1]])
        sense_work(last, strip, [back.at[last - 1], remain.at[last - 1]], [halo_x.at[BACK, 1], halo_x.at[end, 1]])
    sent(end, (0, 1), newest)


def body(back, pert, permit, nodes, weights, owner, sensor, sensor_weight):
    n_px, n_py = lax.axis_size("px"), lax.axis_size("py")
    rows, cols, depth = back.shape
    kinds, probes = nodes.shape
    sensors = sensor_weight.shape[0] * n_px * n_py
    nodes_dev = rows * cols
    f32, bf16 = jnp.float32, jnp.bfloat16
    vmem = pl.BlockSpec(memory_space=pltpu.VMEM)
    smem = pl.BlockSpec(memory_space=pltpu.SMEM)
    block = pltpu.VMEM((rows, cols, depth), f32)
    dma = pltpu.SemaphoreType.DMA
    doubled = pl.pallas_call(
        functools.partial(kernel, n_px, n_py),
        out_shape=jax.ShapeDtypeStruct((rows, cols, depth), f32),
        in_specs=[vmem] * 7 + [smem],
        out_specs=vmem,
        scratch_shapes=[
            pltpu.VMEM((SWEEPS, rows, cols, depth), f32),
            block,
            pltpu.VMEM((rows + 1, cols, depth), f32),
            block, block, block, block, block,
            pltpu.VMEM((EXCHANGES, 2, cols, depth), f32),
            pltpu.VMEM((EXCHANGES, 2, 2, rows, depth), f32),
            pltpu.VMEM((EXCHANGES, 2, 2, rows, depth), f32),
            pltpu.VMEM((depth, 2 * nodes_dev), bf16),
            pltpu.VMEM((nodes_dev, kinds * probes), bf16),
            pltpu.VMEM((2 * nodes_dev, kinds * probes), bf16),
            pltpu.VMEM((depth, kinds * probes), bf16),
            pltpu.VMEM((sensors, probes), bf16),
            pltpu.VMEM((1, probes), f32),
            pltpu.VMEM((n_py, 8, sensors), f32),
            pltpu.VMEM((n_px, 8, sensors), f32),
            dma((EXCHANGES, 2, cols // STRIP)), dma((EXCHANGES, 2, cols // STRIP)),
            dma((EXCHANGES, 2, 2)), dma((EXCHANGES, 2, 2)),
            dma((n_py,)), dma((n_py,)), dma((n_px,)), dma((n_px,)),
        ],
        compiler_params=pltpu.CompilerParams(
            collective_id=0, has_side_effects=True, vmem_limit_bytes=56 * 1024 * 1024
        ),
        cost_estimate=pl.CostEstimate(flops=10_000_000_000, bytes_accessed=4_500_000, transcendentals=0),
    )(
        back, pert, permit, nodes, weights, owner.reshape(1, probes), sensor.reshape(1, probes), sensor_weight
    )
    return -0.5 * doubled


def solution(mesh):
    placed = (
        P("px", "py", None),
        P("px", "py", None),
        P("px", "py", None),
        P(None, ("px", "py")),
        P(None, ("px", "py")),
        P(("px", "py"), None),
        P(("px", "py")),
        P(("px", "py")),
    )
    return jax.shard_map(
        body, mesh=mesh, in_specs=placed, out_specs=P("px", "py", None), check_vma=False
    )
```

time: 73.1 us -> 67 us (0.917)
  Pallas kernels: 70.6 us -> 64.5 us
  other arithmetic: 0 us -> 2.31 us
  local copies, waits for them, and re-layouts: 2.31 us -> 0 us
    pallas_call x1, Pallas kernels: 70.6 us -> 64.5 us  [body(): pl.pallas_call(functools.partial(kernel, n_px, n_py), out_shape=jax.Shape...]
    mul x0 -> x1, other arithmetic: none -> 2.31 us  [body(): return -0.5 * doubled]
    unnamed x1 -> x0, local copies, waits for them, and re-layouts: 2.31 us -> none
where the time goes in v2:
time: 67 us; the launch traced here: 66.8 us
  Pallas kernels  64.5 us (96%)
  other arithmetic  2.31 us (3%)
    pallas_call x1, Pallas kernels, body(): pl.pallas_call(functools.partial(kernel, n_px, n_py), out_shape=jax.Shape...  64.5 us
    mul x1, other arithmetic, body(): return -0.5 * doubled  2.31 us

profile of v2, /device:TPU:0, one launch (start us, length us, event | category | flops | bytes accessed | tf_op | source)
XLA Modules:
  0.0 66.8 jit_solution(4407683079182462306)
XLA Ops:
  0.0 64.5 %shard_map.82 = f32[8,32,1024]{2,1,0:T(8,128)} custom-call(f32[8,32,1024]{2,1,0:T(8,128)} %back.1, f32[8,32,1024]{2,1,0:T(8,128)} %pert.1, f32[8,32,1024]{2,1,0:T(8,128)} %permit.1, s32[4,1024]{1,0:T(4,128)} %nodes.1, f32[4,1024]{1,0:T(4,128)} %weights.1, s32[1,1024]{1,0:T(1,128)} %bitcast.2, s32[1,1024]{1,0:T(1,128)} %bitcast.3, f32[8]{0:T(128)} %sensor_weight.1), custom_call_target="tpu_custom_call" | custom-call | flops 10000000000 | bytes 4500000 | tf_op jit(solution)/shard_map/pallas_call | solution.py:431
  64.5 2.3 %broadcast_multiply_fusion = f32[8,32,1024]{2,1,0:T(8,128)} fusion(f32[8,32,1024]{2,1,0:T(8,128)} %shard_map.82), kind=kLoop, calls=%fused_computation | loop fusion | flops 262144 | bytes 2097152 | tf_op jit(solution)/shard_map/mul | solution.py:463

commit v3 on v2

--- a/solution.py
+++ b/solution.py
@@ -70,7 +70,6 @@
 
     halo_x[...] = jnp.zeros_like(halo_x)
     halo_y[...] = jnp.zeros_like(halo_y)
-    pack_y[...] = jnp.zeros_like(pack_y)
     for side, face in ((0, 0), (1, last)):
         halo_x[BACK, side] = back[face]
         halo_x[PERMIT, side] = -permit[face]
@@ -145,6 +144,8 @@
             start_x(slot, strip, array)
     for strip in order:
         start_x(PERMIT, strip, permit)
+
+    pack_y[TAN:] = jnp.zeros((EXCHANGES - TAN,) + pack_y.shape[1:], jnp.float32)
 
     def hots(kind, _):
         node = nodes[pl.ds(kind, 1), :]
@@ -282,25 +283,22 @@
                 off = off + (coef_yd[at] * yd + coef_yu[at] * yu)
                 off = off + (coef_zd[at] * zd + coef_zu[at] * zu)
                 left = remain[at] - diag[at] * f + off
-                remain[at] = left
-                later[at] = keep * f + gain * left
+                new = keep * f + gain * left
+                if sweep < SWEEPS - 2:
+                    remain[at] = left
+                else:
+                    left = f + new
+                    for index in range(sweep):
+                        left = left + search[(index,) + at]
+                    remain[at] = left
+                if more:
+                    later[at] = new
 
             inner_planes(sweep_work, (slot,), (now,))
             if more:
                 send_inner(slot + 1, later)
             outer_planes(sweep_work, (slot,), (now,), send_outer(slot + 1, later) if more else nothing)
             sent(slot, (0, 1), now)
-
-        def total_plane(x, _):
-            for strip in range(strips):
-                at = (x, slice(strip * STRIP, (strip + 1) * STRIP))
-                total = search[(0,) + at]
-                for index in range(1, SWEEPS):
-                    total = total + search[(index,) + at]
-                remain[at] = total
-            return 0
-
-        lax.fori_loop(0, rows, total_plane, 0)
 
     solve(TAN)
 
@@ -454,7 +452,7 @@
             dma((n_py,)), dma((n_py,)), dma((n_px,)), dma((n_px,)),
         ],
         compiler_params=pltpu.CompilerParams(
-            collective_id=0, has_side_effects=True, vmem_limit_bytes=56 * 1024 * 1024
+            collective_id=0, has_side_effects=True, vmem_limit_bytes=46 * 1024 * 1024
         ),
         cost_estimate=pl.CostEstimate(flops=10_000_000_000, bytes_accessed=4_500_000, transcendentals=0),
     )(

time: 67 us -> 70.5 us (1.052)
  local copies, waits for them, and re-layouts: 0 us -> 7.13 us
  Pallas kernels: 64.5 us -> 61.9 us
  other arithmetic: 2.31 us -> 1.05 us
    unnamed x0 -> x16, local copies, waits for them, and re-layouts: none -> 7.13 us
    pallas_call x1, Pallas kernels: 64.5 us -> 61.9 us  [body(): pl.pallas_call(functools.partial(kernel, n_px, n_py), out_shape=jax.Shape...]
    mul x1, other arithmetic: 2.31 us -> 1.05 us  [body(): return -0.5 * doubled]
where the time goes in v3:
time: 70.5 us; the launch traced here: 70.1 us
  Pallas kernels  61.9 us (88%)
  local copies, waits for them, and re-layouts  7.13 us (10%)
  other arithmetic  1.05 us (1%)
    pallas_call x1, Pallas kernels, body(): pl.pallas_call(functools.partial(kernel, n_px, n_py), out_shape=jax.Shape...  61.9 us
    unnamed x16, local copies, waits for them, and re-layouts  7.13 us

profile of v3, /device:TPU:0, one launch (start us, length us, event | category | flops | bytes accessed | tf_op | source)
XLA Modules:
  0.0 70.1 jit_solution(14282716592931789288)
XLA Ops:
  0.0 0.0 copy-start.7
  0.0 0.7 copy-done.7
  0.7 0.0 copy-start
  0.7 1.2 %copy-done = f32[8,32,1024]{2,1,0:T(8,128)S(1)} copy-done((f32[8,32,1024]{2,1,0:T(8,128)S(1)}, f32[8,32,1024]{2,1,0:T(8,128)}, u32[]{:S(2)}) %copy-start) | copy-done | bytes 1048600
  1.9 0.0 copy-start.1
  1.9 1.2 %copy-done.1 = f32[8,32,1024]{2,1,0:T(8,128)S(1)} copy-done((f32[8,32,1024]{2,1,0:T(8,128)S(1)}, f32[8,32,1024]{2,1,0:T(8,128)}, u32[]{:S(2)}) %copy-start.1) | copy-done | bytes 1048600
  3.1 0.0 copy-start.2
  3.1 1.2 %copy-done.2 = f32[8,32,1024]{2,1,0:T(8,128)S(1)} copy-done((f32[8,32,1024]{2,1,0:T(8,128)S(1)}, f32[8,32,1024]{2,1,0:T(8,128)}, u32[]{:S(2)}) %copy-start.2) | copy-done | bytes 1048600
  4.3 0.0 copy-start.3
  4.3 0.7 %copy-done.3 = s32[4,1024]{1,0:T(4,128)S(1)} copy-done((s32[4,1024]{1,0:T(4,128)S(1)}, s32[4,1024]{1,0:T(4,128)}, u32[]{:S(2)}) %copy-start.3) | copy-done | bytes 16408
  5.0 0.0 copy-start.4
  5.1 0.7 %copy-done.4 = f32[4,1024]{1,0:T(4,128)S(1)} copy-done((f32[4,1024]{1,0:T(4,128)S(1)}, f32[4,1024]{1,0:T(4,128)}, u32[]{:S(2)}) %copy-start.4) | copy-done | bytes 16408
  5.8 0.0 copy-start.5
  5.8 0.7 copy-done.5
  6.5 0.0 copy-start.6
  6.5 0.7 copy-done.6
  7.1 61.9 %shard_map.82 = f32[8,32,1024]{2,1,0:T(8,128)S(1)} custom-call(f32[8,32,1024]{2,1,0:T(8,128)S(1)} %copy-done, f32[8,32,1024]{2,1,0:T(8,128)S(1)} %copy-done.1, f32[8,32,1024]{2,1,0:T(8,128)S(1)} %copy-done.2, s32[4,1024]{1,0:T(4,128)S(1)} %copy-done.3, f32[4,1024]{1,0:T(4,128)S(1)} %copy-done.4, s32[1,1024]{1,0:T(1,128)S(1)} %bitcast.2, ...), custom_call_target="tpu_custom_call" | custom-call | flops 10000000000 | bytes 4500000 | tf_op jit(solution)/shard_map/pallas_call | solution.py:429
  69.0 1.1 %broadcast_multiply_fusion = f32[8,32,1024]{2,1,0:T(8,128)} fusion(f32[8,32,1024]{2,1,0:T(8,128)S(1)} %shard_map.82), kind=kLoop, calls=%fused_computation | loop fusion | flops 262144 | bytes 2097152 | tf_op jit(solution)/shard_map/mul | solution.py:461
Async XLA Ops:
  0.0 0.7 copy-start.7
  0.7 1.2 %copy-start = (f32[8,32,1024]{2,1,0:T(8,128)S(1)}, f32[8,32,1024]{2,1,0:T(8,128)}, u32[]{:S(2)}) copy-start(f32[8,32,1024]{2,1,0:T(8,128)} %back.1) | copy-start | bytes 3145732
  1.9 1.2 %copy-start.1 = (f32[8,32,1024]{2,1,0:T(8,128)S(1)}, f32[8,32,1024]{2,1,0:T(8,128)}, u32[]{:S(2)}) copy-start(f32[8,32,1024]{2,1,0:T(8,128)} %pert.1) | copy-start | bytes 3145732
  3.1 1.2 %copy-start.2 = (f32[8,32,1024]{2,1,0:T(8,128)S(1)}, f32[8,32,1024]{2,1,0:T(8,128)}, u32[]{:S(2)}) copy-start(f32[8,32,1024]{2,1,0:T(8,128)} %permit.1) | copy-start | bytes 3145732
  4.3 0.7 %copy-start.3 = (s32[4,1024]{1,0:T(4,128)S(1)}, s32[4,1024]{1,0:T(4,128)}, u32[]{:S(2)}) copy-start(s32[4,1024]{1,0:T(4,128)} %nodes.1) | copy-start | bytes 49156
  5.0 0.7 %copy-start.4 = (f32[4,1024]{1,0:T(4,128)S(1)}, f32[4,1024]{1,0:T(4,128)}, u32[]{:S(2)}) copy-start(f32[4,1024]{1,0:T(4,128)} %weights.1) | copy-start | bytes 49156
  5.8 0.7 copy-start.5
  6.5 0.7 copy-start.6
